TPU v7x, 32 devices: a whole 2x2x4 slice. The times are simulated.
32 devices in a mesh: lang: 4 (over y, core), pair: 8 (over z, x).
Axes of the slice: x: 2, y: 2, z: 4, core: 2. Of those that a mesh axis runs over, the one named last changes fastest.
Arguments:
- sentences: bfloat16 [128, 128, 1024], P(('lang', 'pair')), may hold values from -16 to 16
- cotangent: bfloat16 [128, 128, 1024], P(('lang', 'pair')), may hold values from -6 to 6
- w_query: bfloat16 [1024, 1024], replicated, may hold values from -0.1875 to 0.1875
- w_key: bfloat16 [1024, 1024], replicated, may hold values from -0.1875 to 0.1875
- w_value: bfloat16 [1024, 1024], replicated, may hold values from -0.1875 to 0.1875
- send_rows: int32 [32, 4, 1], P(('lang', 'pair')), may hold values from 0 to 3
- pair_src: int32 [32, 16], P(('lang', 'pair')), may hold values from 0 to 3
- pair_slot: int32 [32, 16], P(('lang', 'pair')), may hold values from 0 to 3
- pair_valid: int32 [32, 16], P(('lang', 'pair')), may hold values 0 or 1
Outputs:
- attended: bfloat16 [128, 128, 1024], P(('lang', 'pair'))
- grad_sentences: bfloat16 [128, 128, 1024], P(('lang', 'pair'))
- grad_wq: bfloat16 [1024, 1024], replicated
- grad_wk: bfloat16 [1024, 1024], replicated
- grad_wv: bfloat16 [1024, 1024], replicated
All inputs are finite; a program needn't handle non-finite values. No bound on the sum of `pair_valid` on one device may be relied on, other than what follows from the above.
Results may differ from a plain program's by a relative error of at most 0.015.
The roundings to bfloat16 on the way count: a program that leaves them out, or rounds other values in their place, can miss the bound.
Values may be sent and summed in bfloat16 or wider, within the bound.
A program may use at most 128 MiB of HBM per device.

v0:
```python
import jax
import jax.numpy as jnp
from jax import lax
from jax.sharding import PartitionSpec as P

HEADS = 16


def attend_block(q_rows, k_rows, v_rows, g_rows, valid, heads):
    count, length, width = q_rows.shape
    size = width // heads
    scale = size ** (-0.5)
    qh = q_rows.reshape(count, length, heads, size)
    kh = k_rows.reshape(count, length, heads, size)
    vh = v_rows.reshape(count, length, heads, size)
    mult = valid.astype(jnp.float32)[:, None, None, None]
    gh = (
        g_rows.reshape(count, length, heads, size) * valid.astype(jnp.bfloat16)[:, None, None, None]
    )
    scores = jnp.einsum("bqhd,bkhd->bhqk", qh, kh, preferred_element_type=jnp.float32) * scale
    scores = scores - jnp.max(scores, axis=-1, keepdims=True)
    prob = jnp.exp(scores)
    prob = prob / jnp.sum(prob, axis=-1, keepdims=True)
    prob_b = prob.astype(jnp.bfloat16)
    outp = jnp.einsum("bhqk,bkhd->bqhd", prob_b, vh, preferred_element_type=jnp.float32) * mult
    dvalue = jnp.einsum("bhqk,bqhd->bkhd", prob_b, gh, preferred_element_type=jnp.float32)
    dprob = jnp.einsum("bqhd,bkhd->bhqk", gh, vh, preferred_element_type=jnp.float32)
    dscore = prob * (dprob - jnp.sum(prob * dprob, axis=-1, keepdims=True)) * scale
    dscore = dscore.astype(jnp.bfloat16)
    dquery = jnp.einsum("bhqk,bkhd->bqhd", dscore, kh, preferred_element_type=jnp.float32)
    dkey = jnp.einsum("bhqk,bqhd->bkhd", dscore, qh, preferred_element_type=jnp.float32)
    shape = (count, length, width)
    return (outp.reshape(shape), dquery.reshape(shape), dkey.reshape(shape), dvalue.reshape(shape))


def project(rows, weight):
    return (
        jnp.dot(rows.reshape(-1, rows.shape[-1]), weight, preferred_element_type=jnp.float32)
        .astype(jnp.bfloat16)
        .reshape(rows.shape)
    )


def body(sentences, cotangent, w_query, w_key, w_value, send_rows, pair_src, pair_slot, pair_valid):
    sent_dev, length, width = sentences.shape
    n_lang = lax.axis_size("lang")
    n_pair = lax.axis_size("pair")
    cap = send_rows.shape[2]
    slots = n_lang * cap
    listed = send_rows[0].reshape(-1)
    outgoing = jnp.take(sentences, listed, axis=0).reshape(n_lang, cap, length, width)
    received = lax.all_to_all(outgoing, "lang", split_axis=0, concat_axis=0, tiled=True).reshape(
        slots, length, width
    )
    queries = project(sentences, w_query)
    keys = project(received, w_key)
    values = project(received, w_value)
    local_src = pair_src[0]
    pslot = pair_slot[0]
    valid = pair_valid[0]
    block = 4
    zeros_s = jnp.zeros((sent_dev, length, width), jnp.float32)
    zeros_t = jnp.zeros((slots, length, width), jnp.float32)

    def step(i, acc):
        out_acc, dq_acc, dk_acc, dv_acc = acc
        lo = i * block
        locs = lax.dynamic_slice_in_dim(local_src, lo, block)
        chosen = lax.dynamic_slice_in_dim(pslot, lo, block)
        flags = lax.dynamic_slice_in_dim(valid, lo, block)
        outp, dquery, dkey, dvalue = attend_block(
            queries[locs], keys[chosen], values[chosen], cotangent[locs], flags, HEADS
        )
        return (
            out_acc.at[locs].add(outp),
            dq_acc.at[locs].add(dquery),
            dk_acc.at[chosen].add(dkey),
            dv_acc.at[chosen].add(dvalue),
        )

    out_acc, dq_acc, dk_acc, dv_acc = lax.fori_loop(
        0, pair_src.shape[1] // block, step, (zeros_s, zeros_s, zeros_t, zeros_t)
    )
    dq_b = dq_acc.astype(jnp.bfloat16).reshape(-1, width)
    dk_b = dk_acc.astype(jnp.bfloat16).reshape(-1, width)
    dv_b = dv_acc.astype(jnp.bfloat16).reshape(-1, width)
    grad_src = jnp.dot(dq_b, w_query.T, preferred_element_type=jnp.float32).reshape(
        sent_dev, length, width
    )
    dxt = jnp.dot(dk_b, w_key.T, preferred_element_type=jnp.float32) + jnp.dot(
        dv_b, w_value.T, preferred_element_type=jnp.float32
    )
    returned = lax.all_to_all(
        dxt.reshape(n_lang, cap, length, width), "lang", split_axis=0, concat_axis=0, tiled=True
    )
    grad_total = grad_src.at[listed].add(returned.reshape(slots, length, width))
    contract = (((0,), (0,)), ((), ()))
    gwq = lax.dot_general(
        sentences.reshape(-1, width), dq_b, contract, preferred_element_type=jnp.float32
    )
    recv_flat = received.reshape(-1, width)
    gwk = lax.dot_general(recv_flat, dk_b, contract, preferred_element_type=jnp.float32)
    gwv = lax.dot_general(recv_flat, dv_b, contract, preferred_element_type=jnp.float32)
    factor = 1.0 / (sent_dev * n_lang * n_pair * length) ** 0.5
    total_q, total_k, total_v = lax.psum((gwq, gwk, gwv), ("lang", "pair"))
    grad_wq = (total_q * factor).astype(jnp.bfloat16)
    grad_wk = (total_k * factor).astype(jnp.bfloat16)
    grad_wv = (total_v * factor).astype(jnp.bfloat16)
    return (
        out_acc.astype(jnp.bfloat16),
        grad_total.astype(jnp.bfloat16),
        grad_wq,
        grad_wk,
        grad_wv,
    )


def solution(mesh):
    in_specs = (
        P(("lang", "pair"), None, None),
        P(("lang", "pair"), None, None),
        P(),
        P(),
        P(),
        P(("lang", "pair"), None, None),
        P(("lang", "pair"), None),
        P(("lang", "pair"), None),
        P(("lang", "pair"), None),
    )
    out_specs = (P(("lang", "pair"), None, None), P(("lang", "pair"), None, None), P(), P(), P())
    return jax.shard_map(body, mesh=mesh, in_specs=in_specs, out_specs=out_specs, check_vma=False)
```

profile of v0, /device:TPU:0, one launch (start us, length us, event | category | flops | bytes accessed | tf_op | source)
XLA Modules:
  0.0 667.4 jit_solution(17764130741235539002)
XLA Ops:
  20.0 10.3 %all-to-all-done = bf16[4,1,128,1024]{3,2,1,0:T(8,128)(2,1)S(1)} async-done(((bf16[4,1,128,1024]{3,2,1,0:T(8,128)(2,1)}), bf16[4,1,128,1024]{3,2,1,0:T(8,128)(2,1)S(1)}, u32[]{:S(2)}, u32[]{:S(2)}) %all-to-all-start) | async-done | bytes 1048608 | tf_op jit(solution)/shard_map/all_to_all | solution.py:52
  43.2 344.4 %while.19 = (s32[]{:T(128)}, f32[4,128,1024]{2,1,0:T(8,128)}, f32[4,128,1024]{2,1,0:T(8,128)}, f32[4,128,1024]{2,1,0:T(8,128)}, f32[4,128,1024]{2,1,0:T(8,128)},...) while((s32[]{:T(128)}, f32[4,128,1024]{2,1,0:T(8,128)}, ...), condition=%wide.region_8.9_spmd, body=%wide.region_0.8_spmd.sunk | while | flops 831015296 | bytes 126001776 | solution.py:81
  57.8 5.1 fusion.93
  83.9 8.8 %fusion.95 = f32[4,16,64,128]{3,2,1,0:T(8,128)} fusion(bf16[4,128,16,64]{1,3,2,0:T(8,128)(2,1)} %bitcast.110, f32[4,16,128,128]{2,3,1,0:T(8,128)} %fusion.94, f32[4,16,128,128]{2,3,1,0:T(8,128)} %get-tuple-element.348, f32[4,16,128]{2,1,0:T(8,128)S(1)} %get-tuple-element.349), kind=kOutput, calls=%fused_computation.19.clone.1 | convolution fusion | flops 141566080 | bytes 11567104 | tf_op jit(solution)/shard_map/while/body/eval_jaxpr/bhqk,bkhd->bqhd/dot_general | solution.py:30
  100.4 8.5 %fusion.96 = f32[4,16,64,128]{3,2,1,0:T(8,128)} fusion(bf16[4,128,16,64]{1,3,2,0:T(8,128)(2,1)S(1)} %bitcast.108, f32[4,16,128,128]{2,3,1,0:T(8,128)} %fusion.94, f32[4,16,128,128]{2,3,1,0:T(8,128)} %get-tuple-element.348, f32[4,16,128]{2,1,0:T(8,128)S(1)} %get-tuple-element.349), kind=kOutput, calls=%fused_computation.18.clone.1 | convolution fusion | flops 141566080 | bytes 11567104 | tf_op jit(solution)/shard_map/while/body/eval_jaxpr/bhqk,bqhd->bkhd/dot_general | solution.py:31
  116.6 5.1 fusion.97
  124.6 4.9 scatter_fusion.3
  144.0 5.1 fusion.93
  170.1 8.8 %fusion.95 = f32[4,16,64,128]{3,2,1,0:T(8,128)} fusion(bf16[4,128,16,64]{1,3,2,0:T(8,128)(2,1)} %bitcast.110, f32[4,16,128,128]{2,3,1,0:T(8,128)} %fusion.94, f32[4,16,128,128]{2,3,1,0:T(8,128)} %get-tuple-element.348, f32[4,16,128]{2,1,0:T(8,128)S(1)} %get-tuple-element.349), kind=kOutput, calls=%fused_computation.19.clone.1 | convolution fusion | flops 141566080 | bytes 11567104 | tf_op jit(solution)/shard_map/while/body/eval_jaxpr/bhqk,bkhd->bqhd/dot_general | solution.py:30
  186.6 8.5 %fusion.96 = f32[4,16,64,128]{3,2,1,0:T(8,128)} fusion(bf16[4,128,16,64]{1,3,2,0:T(8,128)(2,1)S(1)} %bitcast.108, f32[4,16,128,128]{2,3,1,0:T(8,128)} %fusion.94, f32[4,16,128,128]{2,3,1,0:T(8,128)} %get-tuple-element.348, f32[4,16,128]{2,1,0:T(8,128)S(1)} %get-tuple-element.349), kind=kOutput, calls=%fused_computation.18.clone.1 | convolution fusion | flops 141566080 | bytes 11567104 | tf_op jit(solution)/shard_map/while/body/eval_jaxpr/bhqk,bqhd->bkhd/dot_general | solution.py:31
  197.9 5.0 scatter_fusion.2
  202.9 5.1 fusion.97
  210.9 5.0 scatter_fusion.3
  230.4 5.1 fusion.93
  256.4 8.8 %fusion.95 = f32[4,16,64,128]{3,2,1,0:T(8,128)} fusion(bf16[4,128,16,64]{1,3,2,0:T(8,128)(2,1)} %bitcast.110, f32[4,16,128,128]{2,3,1,0:T(8,128)} %fusion.94, f32[4,16,128,128]{2,3,1,0:T(8,128)} %get-tuple-element.348, f32[4,16,128]{2,1,0:T(8,128)S(1)} %get-tuple-element.349), kind=kOutput, calls=%fused_computation.19.clone.1 | convolution fusion | flops 141566080 | bytes 11567104 | tf_op jit(solution)/shard_map/while/body/eval_jaxpr/bhqk,bkhd->bqhd/dot_general | solution.py:30
  272.7 8.5 %fusion.96 = f32[4,16,64,128]{3,2,1,0:T(8,128)} fusion(bf16[4,128,16,64]{1,3,2,0:T(8,128)(2,1)S(1)} %bitcast.108, f32[4,16,128,128]{2,3,1,0:T(8,128)} %fusion.94, f32[4,16,128,128]{2,3,1,0:T(8,128)} %get-tuple-element.348, f32[4,16,128]{2,1,0:T(8,128)S(1)} %get-tuple-element.349), kind=kOutput, calls=%fused_computation.18.clone.1 | convolution fusion | flops 141566080 | bytes 11567104 | tf_op jit(solution)/shard_map/while/body/eval_jaxpr/bhqk,bqhd->bkhd/dot_general | solution.py:31
  288.8 5.1 fusion.97
  315.9 5.1 fusion.93
  342.0 8.8 %fusion.95 = f32[4,16,64,128]{3,2,1,0:T(8,128)} fusion(bf16[4,128,16,64]{1,3,2,0:T(8,128)(2,1)} %bitcast.110, f32[4,16,128,128]{2,3,1,0:T(8,128)} %fusion.94, f32[4,16,128,128]{2,3,1,0:T(8,128)} %get-tuple-element.348, f32[4,16,128]{2,1,0:T(8,128)S(1)} %get-tuple-element.349), kind=kOutput, calls=%fused_computation.19.clone.1 | convolution fusion | flops 141566080 | bytes 11567104 | tf_op jit(solution)/shard_map/while/body/eval_jaxpr/bhqk,bkhd->bqhd/dot_general | solution.py:30
  358.5 8.5 %fusion.96 = f32[4,16,64,128]{3,2,1,0:T(8,128)} fusion(bf16[4,128,16,64]{1,3,2,0:T(8,128)(2,1)S(1)} %bitcast.108, f32[4,16,128,128]{2,3,1,0:T(8,128)} %fusion.94, f32[4,16,128,128]{2,3,1,0:T(8,128)} %get-tuple-element.348, f32[4,16,128]{2,1,0:T(8,128)S(1)} %get-tuple-element.349), kind=kOutput, calls=%fused_computation.18.clone.1 | convolution fusion | flops 141566080 | bytes 11567104 | tf_op jit(solution)/shard_map/while/body/eval_jaxpr/bhqk,bqhd->bkhd/dot_general | solution.py:31
  374.7 5.1 fusion.97
  417.9 32.7 %all-to-all-done.1 = f32[4,1,128,1024]{3,2,1,0:T(8,128)} async-done(((f32[4,1,128,1024]{3,2,1,0:T(8,128)}), f32[4,1,128,1024]{3,2,1,0:T(8,128)}, u32[]{:S(2)}, u32[]{:S(2)}) %all-to-all-start.1) | async-done | bytes 2097184 | tf_op jit(solution)/shard_map/all_to_all | solution.py:93
  458.2 179.7 %all-reduce.3.cloned.1.call-done = (f32[1024,1024]{0,1:T(8,128)}, f32[1024,1024]{0,1:T(8,128)}, f32[1024,1024]{0,1:T(8,128)}) async-done(((f32[1024,1024]{0,1:T(8,128)}, f32[1024,1024]{0,1:T(8,128)}, f32[1024,1024]{0,1:T(8,128)}), (f32[1024,1024]{0,1:T(8,128)}, f32[1024,1024]{0,1:T(8,128)}, f32[1024,1024]{0,1:T(8,128)})) %all-reduce.3.cloned.1.call-update) | async-done | bytes 12582928 | tf_op jit(solution)/shard_map/psum | solution.py:105
  645.9 6.8 %multiply_convert_fusion.1 = (bf16[1024,1024]{0,1:T(8,128)(2,1)}, bf16[1024,1024]{0,1:T(8,128)(2,1)}) fusion(f32[1024,1024]{0,1:T(8,128)} %get-tuple-element.257, f32[1024,1024]{0,1:T(8,128)} %get-tuple-element.256), kind=kLoop, calls=%fused_computation.45 | loop fusion | flops 4194304 | bytes 12582912 | tf_op jit(solution)/shard_map/convert_element_type | solution.py:108
  (180 shorter events, 298.7 us)
Async XLA Ops:
  7.2 27.4 %copy-start = (bf16[1024,1024]{1,0:T(8,128)(2,1)S(1)}, bf16[1024,1024]{1,0:T(8,128)(2,1)}, u32[]{:S(2)}) copy-start(bf16[1024,1024]{1,0:T(8,128)(2,1)} %param.14) | copy-start | bytes 6291460
  11.6 18.7 %all-to-all-start = ((bf16[4,1,128,1024]{3,2,1,0:T(8,128)(2,1)}), bf16[4,1,128,1024]{3,2,1,0:T(8,128)(2,1)S(1)}, u32[]{:S(2)}, u32[]{:S(2)}) async-start(bf16[4,1,128,1024]{3,2,1,0:T(8,128)(2,1)} %bitcast_select_fusion), calls=%async_computation | async-start | bytes 2097152 | tf_op jit(solution)/shard_map/all_to_all | solution.py:52
  15.9 622.0 %all-reduce.3.cloned.1.call-start = ((), (), s32[]{:S(2)}) async-start(), calls=%async_computation.2 | async-start | bytes 25165824 | tf_op jit(solution)/shard_map/psum | solution.py:105
  31.3 3.3 copy-start.9
  40.0 3.2 copy-start.14
  40.0 3.2 copy-start.15
  40.0 3.2 copy-start.16
  95.6 4.8 copy-start.7
  111.8 4.8 copy-start.1
  124.6 4.9 copy-start.6
  181.8 4.8 copy-start.7
  197.9 5.0 copy-start.1
  210.9 5.0 copy-start.6
  268.1 4.6 copy-start.7
  284.1 4.7 copy-start.1
  296.8 4.7 copy-start.6
  353.7 4.8 copy-start.7
  369.9 4.8 copy-start.1
  382.7 4.8 copy-start.6
  389.9 8.3 %copy-start.11 = (bf16[4,128,1024]{2,1,0:T(8,128)(2,1)}, bf16[4,128,1024]{2,1,0:T(8,128)(2,1)S(1)}, u32[]{:S(2)}) copy-start(bf16[4,128,1024]{2,1,0:T(8,128)(2,1)S(1)} %convert_element_type.67) | copy-start | bytes 3145732
  391.8 3.2 copy-start.10
  406.1 44.5 %all-to-all-start.1 = ((f32[4,1,128,1024]{3,2,1,0:T(8,128)}), f32[4,1,128,1024]{3,2,1,0:T(8,128)}, u32[]{:S(2)}, u32[]{:S(2)}) async-start(f32[4,1,128,1024]{3,2,1,0:T(8,128)} %bitcast.119), calls=%async_computation.1 | async-start | bytes 4194304 | tf_op jit(solution)/shard_map/all_to_all | solution.py:93
  410.7 2.9 copy-start.4
  413.6 37.0 %copy-start.18 = (s32[4]{0:T(128)S(1)}, s32[4]{0:T(128)}, u32[]{:S(2)}) copy-start(s32[4]{0:T(128)} %copy-done.17) | copy-start | bytes 52
  (11 other events, 15.3 us)
Sparse Core Ops, SparseCore 0:
  401.7 236.1 all-reduce.2
where the time goes:
time: 670 us; the launch traced here: 667 us
  waiting for transfers between devices  223 us (33%)
  matrix products  170 us (25%)
  local copies, waits for them, and re-layouts  148 us (22%)
  other arithmetic  103 us (15%)
  between operations  14.2 us (2%)
  starting transfers between devices  8.82 us (1%)
    psum x1, waiting for transfers between devices, body(): total_q, total_k, total_v = lax.psum((gwq, gwk, gwv), ('lang', 'pair'))  180 us
    dot_general x4, matrix products, attend_block(): jnp.einsum('bhqk,bkhd->bqhd', dscore, kh, preferred_element_type=jnp.floa...  35.2 us
    dot_general x4, matrix products, attend_block(): jnp.einsum('bhqk,bqhd->bkhd', dscore, qh, preferred_element_type=jnp.floa...  33.9 us
    all_to_all x1, waiting for transfers between devices, body(): lax.all_to_all(dxt.reshape(n_lang, cap, length, width), 'lang', split_axi...  32.7 us
    sub x4, matrix products, attend_block(): scores = scores - jnp.max(scores, axis=-1, keepdims=True)  20.5 us
    dot_general x4, matrix products, attend_block(): jnp.einsum('bhqk,bqhd->bkhd', prob_b, gh, preferred_element_type=jnp.floa...  20.4 us
    gather x8, local copies, waits for them, and re-layouts, step(): keys[chosen]  20.4 us
    gather x8, local copies, waits for them, and re-layouts, step(): queries[locs]  20.3 us
  transfers between devices with their start and end apart: 3, of which 3 were waited for; matrix products, arithmetic and copies ran while one was open for 3% of the time, Pallas kernels for 0%

commit v1 on v0

v1 whole, which is shorter than its diff:
```python
import jax
import jax.numpy as jnp
from jax import lax
from jax.experimental import pallas as pl
from jax.experimental.pallas import tpu as pltpu
from jax.sharding import PartitionSpec as P

HEADS = 16
LANES = 128
GROUP = 256


def attend_kernel(
    src_ref, slot_ref, valid_ref, q_ref, k_ref, v_ref, g_ref,
    out_ref, dq_ref, dk_ref, dv_ref,
    bd, kv, kvt, out_t, dq_t, dkv, counts,
):
    n_src, length, width = q_ref.shape
    n_slot = k_ref.shape[0]
    size = LANES // 2
    scale = size ** (-0.5)
    blocks = width // LANES
    n_pairs = src_ref.shape[0]
    low = lax.broadcasted_iota(jnp.int32, (length, LANES), 1) < size

    def clear(i, _):
        counts[i] = 0
        return 0

    lax.fori_loop(0, n_src * n_slot, clear, 0)

    def count(j, _):
        key = src_ref[j] * n_slot + slot_ref[j]
        counts[key] = counts[key] + valid_ref[j]
        return 0

    lax.fori_loop(0, n_pairs, count, 0)

    def set_source(s, _):
        for b in range(blocks):
            cols = slice(b * LANES, (b + 1) * LANES)
            q = q_ref[s, :, cols].astype(jnp.float32) * scale
            g = pltpu.roll(g_ref[s, :, cols].astype(jnp.float32), size, 1)
            bd[s, 2 * b, :length] = jnp.where(low, q, 0.0).astype(jnp.bfloat16)
            bd[s, 2 * b, length:] = jnp.where(low, 0.0, g).astype(jnp.bfloat16)
            bd[s, 2 * b + 1, :length] = jnp.where(low, 0.0, q).astype(jnp.bfloat16)
            bd[s, 2 * b + 1, length:] = jnp.where(low, g, 0.0).astype(jnp.bfloat16)
        out_t[s] = jnp.zeros((width, length), jnp.float32)
        dq_t[s] = jnp.zeros((width, length), jnp.float32)
        return 0

    lax.fori_loop(0, n_src, set_source, 0)

    def set_slot(t, _):
        for b in range(blocks):
            cols = slice(b * LANES, (b + 1) * LANES)
            k = k_ref[t, :, cols].astype(jnp.float32)
            v = pltpu.roll(v_ref[t, :, cols].astype(jnp.float32), size, 1)
            even = jnp.where(low, k, v)
            odd = jnp.where(low, v, k)
            kv[t, 2 * b] = even.astype(jnp.bfloat16)
            kv[t, 2 * b + 1] = odd.astype(jnp.bfloat16)
            kvt[t, 2 * b] = even.T.astype(jnp.bfloat16)
            kvt[t, 2 * b + 1] = odd.T.astype(jnp.bfloat16)
            dkv[t, 2 * b] = jnp.zeros((length, LANES), jnp.float32)
            dkv[t, 2 * b + 1] = jnp.zeros((length, LANES), jnp.float32)
        return 0

    lax.fori_loop(0, n_slot, set_slot, 0)

    def combo(i, _):
        times = counts[i]

        @pl.when(times > 0)
        def _():
            s = i // n_slot
            t = i - s * n_slot
            w = times.astype(jnp.float32)
            both = []
            for h in range(2 * blocks):
                both.append(lax.dot_general(
                    kv[t, h], bd[s, h], (((1,), (1,)), ((), ())),
                    preferred_element_type=jnp.float32))
            mixed = []
            for h in range(2 * blocks):
                sc = both[h][:, :length]
                dp = both[h][:, length:]
                e = jnp.exp(sc - jnp.max(sc, axis=0, keepdims=True))
                p = e * (1.0 / jnp.sum(e, axis=0, keepdims=True))
                ds = p * (dp - jnp.sum(p * dp, axis=0, keepdims=True))
                mixed.append(jnp.concatenate(
                    [ds.astype(jnp.bfloat16), p.astype(jnp.bfloat16)], axis=1))
            for h in range(2 * blocks):
                x = mixed[h]
                dkv[t, h] += w * jnp.dot(x, bd[s, h], preferred_element_type=jnp.float32)
                r = jnp.dot(kvt[t, h], x, preferred_element_type=jnp.float32)
                rows = slice(h * size, (h + 1) * size)
                first, second = slice(0, size), slice(size, 2 * size)
                key_rows, value_rows = (first, second) if h % 2 == 0 else (second, first)
                dq_t[s, rows] += w * r[key_rows, :length]
                out_t[s, rows] += w * r[value_rows, length:]

        return 0

    lax.fori_loop(0, n_src * n_slot, combo, 0)

    def put_source(s, _):
        for b in range(blocks):
            cols = slice(b * LANES, (b + 1) * LANES)
            out_ref[s, :, cols] = out_t[s, cols].T.astype(jnp.bfloat16)
            dq_ref[s, :, cols] = (dq_t[s, cols].T * scale).astype(jnp.bfloat16)
        return 0

    lax.fori_loop(0, n_src, put_source, 0)

    def put_slot(t, _):
        for b in range(blocks):
            cols = slice(b * LANES, (b + 1) * LANES)
            even, odd = dkv[t, 2 * b], dkv[t, 2 * b + 1]
            dk_ref[t, :, cols] = jnp.where(low, even, odd).astype(jnp.bfloat16)
            dv_ref[t, :, cols] = pltpu.roll(jnp.where(low, odd, even), size, 1).astype(jnp.bfloat16)
        return 0

    lax.fori_loop(0, n_slot, put_slot, 0)


def attend(group, src, slot, valid, queries, keys, values, cotangent):
    n_src, length, _ = queries.shape
    n_slot = keys.shape[0]
    heads = GROUP // 64
    smem = pl.BlockSpec(memory_space=pltpu.SMEM)

    def cut(rows):
        return pl.BlockSpec((rows, length, GROUP), lambda i: (0, 0, group))

    def whole(rows):
        return pl.BlockSpec((rows, length, GROUP), lambda i: (0, 0, 0))

    def made(rows):
        return jax.ShapeDtypeStruct((rows, length, GROUP), jnp.bfloat16)

    return pl.pallas_call(
        attend_kernel,
        grid=(1,),
        in_specs=[smem, smem, smem, cut(n_src), cut(n_slot), cut(n_slot), cut(n_src)],
        out_specs=[whole(n_src), whole(n_src), whole(n_slot), whole(n_slot)],
        out_shape=[made(n_src), made(n_src), made(n_slot), made(n_slot)],
        scratch_shapes=[
            pltpu.VMEM((n_src, heads, 2 * length, LANES), jnp.bfloat16),
            pltpu.VMEM((n_slot, heads, length, LANES), jnp.bfloat16),
            pltpu.VMEM((n_slot, heads, LANES, length), jnp.bfloat16),
            pltpu.VMEM((n_src, GROUP, length), jnp.float32),
            pltpu.VMEM((n_src, GROUP, length), jnp.float32),
            pltpu.VMEM((n_slot, heads, length, LANES), jnp.float32),
            pltpu.SMEM((n_src * n_slot,), jnp.int32),
        ],
        compiler_params=pltpu.CompilerParams(vmem_limit_bytes=32 * 1024 * 1024),
        cost_estimate=pl.CostEstimate(
            flops=3000000000, bytes_accessed=30000000, transcendentals=1000000),
    )(src, slot, valid, queries, keys, values, cotangent)


def project(rows, weight):
    return (
        jnp.dot(rows.reshape(-1, rows.shape[-1]), weight, preferred_element_type=jnp.float32)
        .astype(jnp.bfloat16)
        .reshape(rows.shape)
    )


def body(sentences, cotangent, w_query, w_key, w_value, send_rows, pair_src, pair_slot, pair_valid):
    sent_dev, length, width = sentences.shape
    n_lang = lax.axis_size("lang")
    n_pair = lax.axis_size("pair")
    cap = send_rows.shape[2]
    slots = n_lang * cap
    axes = ("lang", "pair")
    listed = send_rows[0].reshape(-1)
    outgoing = jnp.take(sentences, listed, axis=0).reshape(n_lang, cap, length, width)
    received = lax.all_to_all(outgoing, "lang", split_axis=0, concat_axis=0, tiled=True).reshape(
        slots, length, width
    )
    queries = project(sentences, w_query)
    keys = project(received, w_key)
    values = project(received, w_value)
    own_flat = sentences.reshape(-1, width)
    recv_flat = received.reshape(-1, width)
    contract = (((0,), (0,)), ((), ()))
    parts, sums = [], []
    for group in range(width // GROUP):
        out, dq, dk, dv = attend(
            group, pair_src[0], pair_slot[0], pair_valid[0], queries, keys, values, cotangent)
        parts.append((out, dq, dk, dv))
        gwq = lax.dot_general(own_flat, dq.reshape(-1, GROUP), contract,
                              preferred_element_type=jnp.float32)
        gwk = lax.dot_general(recv_flat, dk.reshape(-1, GROUP), contract,
                              preferred_element_type=jnp.float32)
        gwv = lax.dot_general(recv_flat, dv.reshape(-1, GROUP), contract,
                              preferred_element_type=jnp.float32)
        sums.append(lax.psum_scatter(
            jnp.concatenate([gwq, gwk, gwv], axis=1), axes, scatter_dimension=0, tiled=True))
    attended, dq_b, dk_b, dv_b = (
        jnp.concatenate([part[i] for part in parts], axis=2) for i in range(4))
    flat = (-1, width)
    dxt = jnp.dot(dk_b.reshape(flat), w_key.T, preferred_element_type=jnp.float32) + jnp.dot(
        dv_b.reshape(flat), w_value.T, preferred_element_type=jnp.float32
    )
    returned = lax.all_to_all(
        dxt.reshape(n_lang, cap, length, width), "lang", split_axis=0, concat_axis=0, tiled=True
    )
    grad_src = jnp.dot(dq_b.reshape(flat), w_query.T, preferred_element_type=jnp.float32).reshape(
        sent_dev, length, width
    )
    pick = (listed[None, :] == jnp.arange(sent_dev, dtype=listed.dtype)[:, None])
    returned = returned.reshape(slots, length, width)
    grad_total = grad_src
    for t in range(slots):
        grad_total = grad_total + jnp.where(pick[:, t, None, None], returned[t][None], 0.0)
    factor = 1.0 / (sent_dev * n_lang * n_pair * length) ** 0.5
    grads = []
    for i in range(3):
        mine = jnp.concatenate([total[:, i * GROUP:(i + 1) * GROUP] for total in sums], axis=1)
        grads.append(lax.all_gather(
            (mine * factor).astype(jnp.bfloat16), axes, axis=0, tiled=True))
    return (attended, grad_total.astype(jnp.bfloat16), *grads)


def solution(mesh):
    in_specs = (
        P(("lang", "pair"), None, None),
        P(("lang", "pair"), None, None),
        P(),
        P(),
        P(),
        P(("lang", "pair"), None, None),
        P(("lang", "pair"), None),
        P(("lang", "pair"), None),
        P(("lang", "pair"), None),
    )
    out_specs = (P(("lang", "pair"), None, None), P(("lang", "pair"), None, None), P(), P(), P())
    return jax.shard_map(body, mesh=mesh, in_specs=in_specs, out_specs=out_specs, check_vma=False)
```

time: 670 us -> 662 us (0.988)
  waiting for transfers between devices: 223 us -> 517 us
  matrix products: 170 us -> 18.9 us
  local copies, waits for them, and re-layouts: 148 us -> 51.4 us
  other arithmetic: 103 us -> 17.9 us
  Pallas kernels: 0 us -> 32 us
    unnamed x1 -> x11, waiting for transfers between devices: 0.02 us -> 353 us
    psum x1 -> x0, waiting for transfers between devices: 180 us -> none  [body(): total_q, total_k, total_v = lax.psum((gwq, gwk, gwv), ('lang', 'pair'))]
    dot_general x26 -> x15, matrix products: 140 us -> 12.2 us  [the longest x1 2.62 us: body(): jnp.dot(dv_b.reshape(flat), w_value.T, preferred_element_type=jnp.float32)]
    all_gather x0 -> x3, waiting for transfers between devices: none -> 128 us  [body(): lax.all_gather((mine * factor).astype(jnp.bfloat16), axes, axis=0, tiled=...]
    scatter-add x17 -> x0, other arithmetic: 81.5 us -> none  [the longest x4 19.4 us: step(): dv_acc.at[chosen].add(dvalue)]
    gather x32 -> x0, local copies, waits for them, and re-layouts: 73.8 us -> none  [the longest x8 20.4 us: step(): keys[chosen]]
    reshape x16 -> x0, local copies, waits for them, and re-layouts: 46.6 us -> none  [the longest x4 11.7 us: attend_block(): dkey.reshape(shape)]
    pallas_call x0 -> x4, Pallas kernels: none -> 32 us  [attend(): pl.pallas_call(attend_kernel, grid=(1,), in_specs=[smem, smem, smem, cut(...]
  transfers between devices with their start and end apart: 3 -> 9, of which waited for: 3 -> 9; matrix products, arithmetic and copies ran while one was open for 3% -> 7% of each run, Pallas kernels for 0% -> 4%
where the time goes in v1:
time: 662 us; the launch traced here: 661 us
  waiting for transfers between devices  517 us (78%)
  local copies, waits for them, and re-layouts  51.4 us (8%)
  Pallas kernels  32 us (5%)
  matrix products  18.9 us (3%)
  other arithmetic  17.9 us (3%)
  between operations  14.7 us (2%)
  starting transfers between devices  9.27 us (1%)
    unnamed x11, waiting for transfers between devices  353 us
    all_gather x3, waiting for transfers between devices, body(): lax.all_gather((mine * factor).astype(jnp.bfloat16), axes, axis=0, tiled=...  128 us
    unnamed x115, local copies, waits for them, and re-layouts  41.8 us
    pallas_call x4, Pallas kernels, attend(): pl.pallas_call(attend_kernel, grid=(1,), in_specs=[smem, smem, smem, cut(...  32 us
    all_to_all x1, waiting for transfers between devices, body(): lax.all_to_all(dxt.reshape(n_lang, cap, length, width), 'lang', split_axi...  25.5 us
  transfers between devices with their start and end apart: 9, of which 9 were waited for; matrix products, arithmetic and copies ran while one was open for 7% of the time, Pallas kernels for 4%

profile of v1, /device:TPU:0, one launch (start us, length us, event | category | flops | bytes accessed | tf_op | source)
XLA Modules:
  0.0 661.0 jit_solution(14379293281234236732)
XLA Ops:
  11.6 4.2 all-to-all-start
  15.9 4.1 convolution_convert_fusion.2
  20.0 10.3 %all-to-all-done = bf16[4,1,128,1024]{3,2,1,0:T(8,128)(2,1)S(1)} async-done(((bf16[4,1,128,1024]{3,2,1,0:T(8,128)(2,1)}), bf16[4,1,128,1024]{3,2,1,0:T(8,128)(2,1)S(1)}, u32[]{:S(2)}, u32[]{:S(2)}) %all-to-all-start) | async-done | bytes 1048608 | tf_op jit(solution)/shard_map/all_to_all | solution.py:180
  34.3 8.0 %shard_map.131 = (bf16[4,128,256]{2,1,0:T(8,128)(2,1)S(1)}, bf16[4,128,256]{2,1,0:T(8,128)(2,1)S(1)}, bf16[4,128,256]{2,1,0:T(8,128)(2,1)S(1)}, bf16[4,128,256]{2,1,0:T(8,128)(2,1)S(1)}) custom-call(s32[16]{0:T(128)S(1)} %bitcast.112, s32[16]{0:T(128)S(1)} %bitcast.116, s32[16]{0:T(128)S(1)} %bitcast.120, bf16[4,128,1024]{2,1,0:T(8,128)(2,1)S(1)} %bitcast.124, ...), custom_call_target="tpu_custom_call" | custom-call | flops 3000000000 | bytes 30000000 | tf_op jit(solution)/shard_map/pallas_call | solution.py:142
  46.3 3.5 copy.49
  54.8 8.0 %shard_map.130 = (bf16[4,128,256]{2,1,0:T(8,128)(2,1)S(1)}, bf16[4,128,256]{2,1,0:T(8,128)(2,1)S(1)}, bf16[4,128,256]{2,1,0:T(8,128)(2,1)S(1)}, bf16[4,128,256]{2,1,0:T(8,128)(2,1)S(1)}) custom-call(s32[16]{0:T(128)S(1)} %bitcast.113, s32[16]{0:T(128)S(1)} %bitcast.117, s32[16]{0:T(128)S(1)} %bitcast.121, bf16[4,128,1024]{2,1,0:T(8,128)(2,1)S(1)} %bitcast.125, ...), custom_call_target="tpu_custom_call" | custom-call | flops 3000000000 | bytes 30000000 | tf_op jit(solution)/shard_map/pallas_call | solution.py:142
  67.4 3.6 copy.47
  76.1 8.0 %shard_map.129 = (bf16[4,128,256]{2,1,0:T(8,128)(2,1)S(1)}, bf16[4,128,256]{2,1,0:T(8,128)(2,1)S(1)}, bf16[4,128,256]{2,1,0:T(8,128)(2,1)S(1)}, bf16[4,128,256]{2,1,0:T(8,128)(2,1)S(1)}) custom-call(s32[16]{0:T(128)S(1)} %bitcast.114, s32[16]{0:T(128)S(1)} %bitcast.118, s32[16]{0:T(128)S(1)} %bitcast.122, bf16[4,128,1024]{2,1,0:T(8,128)(2,1)S(1)} %bitcast.126, ...), custom_call_target="tpu_custom_call" | custom-call | flops 3000000000 | bytes 30000000 | tf_op jit(solution)/shard_map/pallas_call | solution.py:142
  86.7 2.2 pad_maximum_fusion.1
  88.9 3.6 copy.45
  97.7 8.0 %shard_map.128 = (bf16[4,128,256]{2,1,0:T(8,128)(2,1)S(1)}, bf16[4,128,256]{2,1,0:T(8,128)(2,1)S(1)}, bf16[4,128,256]{2,1,0:T(8,128)(2,1)S(1)}, bf16[4,128,256]{2,1,0:T(8,128)(2,1)S(1)}) custom-call(s32[16]{0:T(128)S(1)} %bitcast.115, s32[16]{0:T(128)S(1)} %bitcast.119, s32[16]{0:T(128)S(1)} %bitcast.123, bf16[4,128,1024]{2,1,0:T(8,128)(2,1)S(1)} %bitcast.127, ...), custom_call_target="tpu_custom_call" | custom-call | flops 3000000000 | bytes 30000000 | tf_op jit(solution)/shard_map/pallas_call | solution.py:142
  110.4 3.7 copy.43
  114.2 39.6 %reduce-scatter.19.cloned.1.call-done = f32[32,768]{1,0:T(8,128)} async-done(((f32[1024,768]{1,0:T(8,128)}), f32[32,768]{1,0:T(8,128)}) %reduce-scatter.19.cloned.1.call-update) | async-done | bytes 98320
  155.1 104.5 %reduce-scatter.17.cloned.1.call-done = f32[32,768]{1,0:T(8,128)} async-done(((f32[1024,768]{1,0:T(8,128)}), f32[32,768]{1,0:T(8,128)}) %reduce-scatter.17.cloned.1.call-update) | async-done | bytes 98320
  261.1 104.5 %reduce-scatter.15.cloned.1.call-done = f32[32,768]{1,0:T(8,128)} async-done(((f32[1024,768]{1,0:T(8,128)}), f32[32,768]{1,0:T(8,128)}) %reduce-scatter.15.cloned.1.call-update) | async-done | bytes 98320
  367.0 104.5 %reduce-scatter.13.cloned.1.call-done = f32[32,768]{1,0:T(8,128)} async-done(((f32[1024,768]{1,0:T(8,128)}), f32[32,768]{1,0:T(8,128)}) %reduce-scatter.13.cloned.1.call-update) | async-done | bytes 98320
  480.3 2.6 convolution_add_fusion
  483.0 4.6 all-to-all-start.1
  488.8 25.5 %all-to-all-done.1 = f32[4,1,128,1024]{3,2,1,0:T(8,128)} async-done(((f32[4,1,128,1024]{3,2,1,0:T(8,128)}), f32[4,1,128,1024]{3,2,1,0:T(8,128)}, u32[]{:S(2)}, u32[]{:S(2)}) %all-to-all-start.1) | async-done | bytes 2097184 | tf_op jit(solution)/shard_map/all_to_all | solution.py:208
  516.8 2.6 add_convert_fusion
  519.4 11.3 %all-gather.4.cloned.1.call-done = bf16[1024,1024]{1,0:T(8,128)(2,1)} async-done(((bf16[32,1024]{1,0:T(8,128)(2,1)}), bf16[1024,1024]{1,0:T(8,128)(2,1)}) %all-gather.4.cloned.1.call-update) | async-done | bytes 2097168 | tf_op jit(solution)/shard_map/all_gather | solution.py:223
  530.7 58.2 %all-gather.6.cloned.1.call-done = bf16[1024,1024]{1,0:T(8,128)(2,1)} async-done(((bf16[32,1024]{1,0:T(8,128)(2,1)}), bf16[1024,1024]{1,0:T(8,128)(2,1)}) %all-gather.6.cloned.1.call-update) | async-done | bytes 2097168 | tf_op jit(solution)/shard_map/all_gather | solution.py:223
  588.9 58.4 %all-gather.8.cloned.1.call-done = bf16[1024,1024]{1,0:T(8,128)(2,1)} async-done(((bf16[32,1024]{1,0:T(8,128)(2,1)}), bf16[1024,1024]{1,0:T(8,128)(2,1)}) %all-gather.8.cloned.1.call-update) | async-done | bytes 2097168 | tf_op jit(solution)/shard_map/all_gather | solution.py:223
  647.3 3.2 copy.66
  (159 shorter events, 59.4 us)
Async XLA Ops:
  7.2 23.2 %copy-start = (bf16[1024,1024]{1,0:T(8,128)(2,1)S(1)}, bf16[1024,1024]{1,0:T(8,128)(2,1)}, u32[]{:S(2)}) copy-start(bf16[1024,1024]{1,0:T(8,128)(2,1)} %param.12) | copy-start | bytes 6291460
  11.6 18.7 %all-to-all-start = ((bf16[4,1,128,1024]{3,2,1,0:T(8,128)(2,1)}), bf16[4,1,128,1024]{3,2,1,0:T(8,128)(2,1)S(1)}, u32[]{:S(2)}, u32[]{:S(2)}) async-start(bf16[4,1,128,1024]{3,2,1,0:T(8,128)(2,1)} %bitcast_select_fusion), calls=%async_computation | async-start | bytes 2097152 | tf_op jit(solution)/shard_map/all_to_all | solution.py:180
  15.9 137.8 %reduce-scatter.19.cloned.1.call-start = ((), (), s32[]{:S(2)}) async-start(), calls=%async_computation.12 | async-start | bytes 3244032
  33.6 8.7 %copy-start.35 = (bf16[512,1024]{1,0:T(8,128)(2,1)}, bf16[512,1024]{1,0:T(8,128)(2,1)S(1)}, u32[]{:S(2)}) copy-start(bf16[512,1024]{1,0:T(8,128)(2,1)S(1)} %convolution_convert_fusion) | copy-start | bytes 3145732
  34.3 8.0 %copy-start.40 = (bf16[4,1,128,1024]{3,2,1,0:T(8,128)(2,1)S(1)}, bf16[4,1,128,1024]{3,2,1,0:T(8,128)(2,1)}, u32[]{:S(2)}) copy-start(bf16[4,1,128,1024]{3,2,1,0:T(8,128)(2,1)} %copy-done.39) | copy-start | bytes 3145732
  49.9 209.8 %reduce-scatter.17.cloned.1.call-start = ((), (), s32[]{:S(2)}) async-start(), calls=%async_computation.11 | async-start | bytes 3244032
  54.8 8.1 %copy-start.45 = (bf16[4,128,1024]{2,1,0:T(8,128)(2,1)S(1)}, bf16[4,128,1024]{2,1,0:T(8,128)(2,1)}, u32[]{:S(2)}) copy-start(bf16[4,128,1024]{2,1,0:T(8,128)(2,1)} %param.9) | copy-start | bytes 3145732
  71.1 294.5 %reduce-scatter.15.cloned.1.call-start = ((), (), s32[]{:S(2)}) async-start(), calls=%async_computation.10 | async-start | bytes 3244032
  76.1 8.1 %copy-start.46 = (bf16[4,128,1024]{2,1,0:T(8,128)(2,1)S(1)}, bf16[4,128,1024]{2,1,0:T(8,128)(2,1)}, u32[]{:S(2)}) copy-start(bf16[4,128,1024]{2,1,0:T(8,128)(2,1)} %param.9) | copy-start | bytes 3145732
  92.6 378.9 %reduce-scatter.13.cloned.1.call-start = ((), (), s32[]{:S(2)}) async-start(), calls=%async_computation.9 | async-start | bytes 3244032
  97.7 8.1 %copy-start.47 = (bf16[4,128,1024]{2,1,0:T(8,128)(2,1)S(1)}, bf16[4,128,1024]{2,1,0:T(8,128)(2,1)}, u32[]{:S(2)}) copy-start(bf16[4,128,1024]{2,1,0:T(8,128)(2,1)} %param.9) | copy-start | bytes 3145732
  114.1 416.5 %all-gather.4.cloned.1.call-start = ((), (), s32[]{:S(2)}) async-start(), calls=%async_computation.6 | async-start | bytes 2162688 | tf_op jit(solution)/shard_map/all_gather | solution.py:223
  474.4 114.5 %all-gather.6.cloned.1.call-start = ((), (), s32[]{:S(2)}) async-start(), calls=%async_computation.7 | async-start | bytes 2162688 | tf_op jit(solution)/shard_map/all_gather | solution.py:223
  475.9 171.4 %all-gather.8.cloned.1.call-start = ((), (), s32[]{:S(2)}) async-start(), calls=%async_computation.8 | async-start | bytes 2162688 | tf_op jit(solution)/shard_map/all_gather | solution.py:223
  482.9 4.6 copy-start.53
  482.9 4.7 copy-start.13
  482.9 4.7 copy-start.15
  482.9 4.7 copy-start.17
  482.9 4.7 copy-start.19
  483.0 31.3 %all-to-all-start.1 = ((f32[4,1,128,1024]{3,2,1,0:T(8,128)}), f32[4,1,128,1024]{3,2,1,0:T(8,128)}, u32[]{:S(2)}, u32[]{:S(2)}) async-start(f32[4,1,128,1024]{3,2,1,0:T(8,128)} %bitcast.147), calls=%async_computation.1 | async-start | bytes 4194304 | tf_op jit(solution)/shard_map/all_to_all | solution.py:208
  488.8 27.6 %copy-start.5 = (bf16[4,128,256]{2,1,0:T(8,128)(2,1)S(1)}, bf16[4,128,256]{2,1,0:T(8,128)(2,1)}, u32[]{:S(2)}) copy-start(bf16[4,128,256]{2,1,0:T(8,128)(2,1)} %copy-done.4) | copy-start | bytes 786436
  488.8 27.6 %copy-start.7 = (bf16[4,128,256]{2,1,0:T(8,128)(2,1)S(1)}, bf16[4,128,256]{2,1,0:T(8,128)(2,1)}, u32[]{:S(2)}) copy-start(bf16[4,128,256]{2,1,0:T(8,128)(2,1)} %copy-done.6) | copy-start | bytes 786436
  488.8 27.6 %copy-start.9 = (bf16[4,128,256]{2,1,0:T(8,128)(2,1)S(1)}, bf16[4,128,256]{2,1,0:T(8,128)(2,1)}, u32[]{:S(2)}) copy-start(bf16[4,128,256]{2,1,0:T(8,128)(2,1)} %copy-done.8) | copy-start | bytes 786436
  488.8 27.6 %copy-start.11 = (bf16[4,128,256]{2,1,0:T(8,128)(2,1)S(1)}, bf16[4,128,256]{2,1,0:T(8,128)(2,1)}, u32[]{:S(2)}) copy-start(bf16[4,128,256]{2,1,0:T(8,128)(2,1)} %copy-done.10) | copy-start | bytes 786436
  (39 other events, 63.9 us)
Sparse Core Ops, SparseCore 0:
  50.0 103.6 reduce-scatter.18
  159.2 100.4 reduce-scatter.16
  265.1 100.4 reduce-scatter.14
  370.9 100.5 reduce-scatter.12
  474.9 55.7 all-gather.3
  533.5 55.3 all-gather.5
  591.9 55.3 all-gather.7

commit v2 on v1

--- a/solution.py
+++ b/solution.py
@@ -124,26 +124,23 @@
     lax.fori_loop(0, n_slot, put_slot, 0)
 
 
-def attend(group, src, slot, valid, queries, keys, values, cotangent):
-    n_src, length, _ = queries.shape
+def attend(src, slot, valid, queries, keys, values, cotangent):
+    n_src, length, width = queries.shape
     n_slot = keys.shape[0]
-    heads = GROUP // 64
+    heads = 2 * GROUP // LANES
     smem = pl.BlockSpec(memory_space=pltpu.SMEM)
 
     def cut(rows):
-        return pl.BlockSpec((rows, length, GROUP), lambda i: (0, 0, group))
-
-    def whole(rows):
-        return pl.BlockSpec((rows, length, GROUP), lambda i: (0, 0, 0))
+        return pl.BlockSpec((rows, length, GROUP), lambda i: (0, 0, i))
 
     def made(rows):
-        return jax.ShapeDtypeStruct((rows, length, GROUP), jnp.bfloat16)
+        return jax.ShapeDtypeStruct((rows, length, width), jnp.bfloat16)
 
     return pl.pallas_call(
         attend_kernel,
-        grid=(1,),
+        grid=(width // GROUP,),
         in_specs=[smem, smem, smem, cut(n_src), cut(n_slot), cut(n_slot), cut(n_src)],
-        out_specs=[whole(n_src), whole(n_src), whole(n_slot), whole(n_slot)],
+        out_specs=[cut(n_src), cut(n_src), cut(n_slot), cut(n_slot)],
         out_shape=[made(n_src), made(n_src), made(n_slot), made(n_slot)],
         scratch_shapes=[
             pltpu.VMEM((n_src, heads, 2 * length, LANES), jnp.bfloat16),
@@ -156,7 +153,7 @@
         ],
         compiler_params=pltpu.CompilerParams(vmem_limit_bytes=32 * 1024 * 1024),
         cost_estimate=pl.CostEstimate(
-            flops=3000000000, bytes_accessed=30000000, transcendentals=1000000),
+            flops=12000000000, bytes_accessed=30000000, transcendentals=4000000),
     )(src, slot, valid, queries, keys, values, cotangent)
 
 
@@ -166,6 +163,19 @@
         .astype(jnp.bfloat16)
         .reshape(rows.shape)
     )
+
+
+AXES = ("lang", "pair")
+
+
+def swap(x, bit):
+    n = lax.axis_size("lang") * lax.axis_size("pair")
+    return lax.ppermute(x, AXES, [(i, i ^ (1 << bit)) for i in range(n)])
+
+
+def half(x, which, axis=0):
+    rows = x.shape[axis] // 2
+    return lax.dynamic_slice_in_dim(x, which * rows, rows, axis)
 
 
 def body(sentences, cotangent, w_query, w_key, w_value, send_rows, pair_src, pair_slot, pair_valid):
@@ -174,55 +184,85 @@
     n_pair = lax.axis_size("pair")
     cap = send_rows.shape[2]
     slots = n_lang * cap
-    axes = ("lang", "pair")
-    listed = send_rows[0].reshape(-1)
-    outgoing = jnp.take(sentences, listed, axis=0).reshape(n_lang, cap, length, width)
-    received = lax.all_to_all(outgoing, "lang", split_axis=0, concat_axis=0, tiled=True).reshape(
-        slots, length, width
-    )
+    lang = lax.axis_index("lang")
+    me = lang * n_pair + lax.axis_index("pair")
+    pair_bits = n_pair.bit_length() - 1
+    lang_bits = n_lang.bit_length() - 1
+    core = pair_bits
+    low = list(range(pair_bits // 2))
+    high = list(range(pair_bits // 2, pair_bits))
+    upper = list(range(pair_bits + 1, pair_bits + lang_bits))
+
+    def exchange(x, d):
+        return lax.ppermute(x, "lang", [(i, i ^ d) for i in range(n_lang)])
+
+    listed = [lax.dynamic_index_in_dim(send_rows[0], lang ^ d, 0, False) for d in range(n_lang)]
+    received = []
+    for d in range(n_lang):
+        block = jnp.take(sentences, listed[d], axis=0)
+        received.append(exchange(block, d) if d else block)
+    received = jnp.concatenate(received, axis=0)
+    slot = pair_slot[0]
+    slot = ((slot // cap) ^ lang) * cap + slot % cap
+
     queries = project(sentences, w_query)
     keys = project(received, w_key)
     values = project(received, w_value)
-    own_flat = sentences.reshape(-1, width)
-    recv_flat = received.reshape(-1, width)
+    attended, dq, dk, dv = attend(
+        pair_src[0], slot, pair_valid[0], queries, keys, values, cotangent)
+    flat = (-1, width)
+    dq_b, dk_b, dv_b = dq.reshape(flat), dk.reshape(flat), dv.reshape(flat)
+
+    my = {b: (me >> b) & 1 for b in range(pair_bits + lang_bits)}
+    own_flat = sentences.reshape(flat)
+    recv_flat = received.reshape(flat)
     contract = (((0,), (0,)), ((), ()))
-    parts, sums = [], []
-    for group in range(width // GROUP):
-        out, dq, dk, dv = attend(
-            group, pair_src[0], pair_slot[0], pair_valid[0], queries, keys, values, cotangent)
-        parts.append((out, dq, dk, dv))
-        gwq = lax.dot_general(own_flat, dq.reshape(-1, GROUP), contract,
-                              preferred_element_type=jnp.float32)
-        gwk = lax.dot_general(recv_flat, dk.reshape(-1, GROUP), contract,
-                              preferred_element_type=jnp.float32)
-        gwv = lax.dot_general(recv_flat, dv.reshape(-1, GROUP), contract,
-                              preferred_element_type=jnp.float32)
-        sums.append(lax.psum_scatter(
-            jnp.concatenate([gwq, gwk, gwv], axis=1), axes, scatter_dimension=0, tiled=True))
-    attended, dq_b, dk_b, dv_b = (
-        jnp.concatenate([part[i] for part in parts], axis=2) for i in range(4))
-    flat = (-1, width)
-    dxt = jnp.dot(dk_b.reshape(flat), w_key.T, preferred_element_type=jnp.float32) + jnp.dot(
-        dv_b.reshape(flat), w_value.T, preferred_element_type=jnp.float32
-    )
-    returned = lax.all_to_all(
-        dxt.reshape(n_lang, cap, length, width), "lang", split_axis=0, concat_axis=0, tiled=True
-    )
-    grad_src = jnp.dot(dq_b.reshape(flat), w_query.T, preferred_element_type=jnp.float32).reshape(
+
+    def outer(rows, d):
+        return lax.dot_general(rows, d, contract, preferred_element_type=jnp.float32)
+
+    jobs = [
+        (recv_flat, dv_b, high + low + upper),
+        (recv_flat, dk_b, upper + high + low),
+        (own_flat, dq_b, low + upper + high),
+    ]
+    got = [swap(outer(half(rows, 1 - my[core], 1), d), core) for rows, d, _ in jobs]
+    kept = [outer(half(rows, my[core], 1), d) for rows, d, _ in jobs]
+
+    dxt = jnp.dot(dk_b, w_key.T, preferred_element_type=jnp.float32) + jnp.dot(
+        dv_b, w_value.T, preferred_element_type=jnp.float32
+    )
+    dxt = dxt.reshape(n_lang, cap, length, width)
+    returned = [exchange(dxt[d], d) if d else dxt[d] for d in range(n_lang)]
+
+    for step in range(len(jobs[0][2])):
+        sent = []
+        for j, (_, _, order) in enumerate(jobs):
+            b = order[step]
+            sent.append(swap(half(kept[j], 1 - my[b]) + half(got[j], 1 - my[b]), b))
+        for j, (_, _, order) in enumerate(jobs):
+            b = order[step]
+            kept[j] = half(kept[j], my[b]) + half(got[j], my[b])
+        got = sent
+    factor = 1.0 / (sent_dev * n_lang * n_pair * length) ** 0.5
+    whole = [((kept[j] + got[j]) * factor).astype(jnp.bfloat16) for j in range(3)]
+    for step in reversed(range(-1, len(jobs[0][2]))):
+        order = [core if step < 0 else job[2][step] for job in jobs]
+        other = [swap(whole[j], order[j]) for j in range(3)]
+        for j in range(3):
+            first = my[order[j]] == 0
+            whole[j] = jnp.concatenate([
+                jnp.where(first, whole[j], other[j]), jnp.where(first, other[j], whole[j])], axis=0)
+
+    grad_total = jnp.dot(dq_b, w_query.T, preferred_element_type=jnp.float32).reshape(
         sent_dev, length, width
     )
-    pick = (listed[None, :] == jnp.arange(sent_dev, dtype=listed.dtype)[:, None])
-    returned = returned.reshape(slots, length, width)
-    grad_total = grad_src
-    for t in range(slots):
-        grad_total = grad_total + jnp.where(pick[:, t, None, None], returned[t][None], 0.0)
-    factor = 1.0 / (sent_dev * n_lang * n_pair * length) ** 0.5
-    grads = []
-    for i in range(3):
-        mine = jnp.concatenate([total[:, i * GROUP:(i + 1) * GROUP] for total in sums], axis=1)
-        grads.append(lax.all_gather(
-            (mine * factor).astype(jnp.bfloat16), axes, axis=0, tiled=True))
-    return (attended, grad_total.astype(jnp.bfloat16), *grads)
+    owner = jnp.arange(sent_dev, dtype=jnp.int32)
+    for d in range(n_lang):
+        for c in range(cap):
+            pick = (owner == listed[d][c])[:, None, None]
+            grad_total = grad_total + jnp.where(pick, returned[d][c][None], 0.0)
+    return (attended, grad_total.astype(jnp.bfloat16), whole[2], whole[1], whole[0])
 
 
 def solution(mesh):

time: 662 us -> 239 us (0.36)
  waiting for transfers between devices: 517 us -> 87 us
  starting transfers between devices: 9.27 us -> 57.4 us
  local copies, waits for them, and re-layouts: 51.4 us -> 4.03 us
  other arithmetic: 17.9 us -> 28.4 us
    unnamed x11 -> x0, waiting for transfers between devices: 353 us -> none
    all_gather x3 -> x0, waiting for transfers between devices: 128 us -> none  [body(): lax.all_gather((mine * factor).astype(jnp.bfloat16), axes, axis=0, tiled=...]
    ppermute x0 -> x36, waiting for transfers between devices: none -> 87 us  [the longest x30 78.7 us: swap(): return lax.ppermute(x, AXES, [(i, i ^ 1 << bit) for i in range(n)])]
    ppermute x0 -> x36, starting transfers between devices: none -> 57.4 us  [the longest x30 51.3 us: swap(): return lax.ppermute(x, AXES, [(i, i ^ 1 << bit) for i in range(n)])]
    unnamed x115 -> x44, local copies, waits for them, and re-layouts: 41.8 us -> 2.27 us
    all_to_all x2 -> x0, waiting for transfers between devices: 35.8 us -> none  [the longest x1 25.5 us: body(): lax.all_to_all(dxt.reshape(n_lang, cap, length, width), 'lang', split_axi...]
    add x0 -> x12, other arithmetic: none -> 14.1 us  [the longest x9 14.1 us: body(): kept[j] = half(kept[j], my[b]) + half(got[j], my[b])]
    all_to_all x2 -> x0, starting transfers between devices: 8.83 us -> none  [the longest x1 4.6 us: body(): lax.all_to_all(dxt.reshape(n_lang, cap, length, width), 'lang', split_axi...]
  transfers between devices with their start and end apart: 9 -> 36, of which waited for: 9 -> 18; matrix products, arithmetic and copies ran while one was open for 7% -> 17% of each run, Pallas kernels for 4% -> 0%
where the time goes in v2:
time: 239 us; the launch traced here: 238 us
  waiting for transfers between devices  87 us (36%)
  starting transfers between devices  57.4 us (24%)
  Pallas kernels  29.8 us (12%)
  other arithmetic  28.4 us (12%)
  matrix products  22.7 us (9%)
  between operations  8.87 us (4%)
  local copies, waits for them, and re-layouts  4.03 us (2%)
    ppermute x30, waiting for transfers between devices, swap(): return lax.ppermute(x, AXES, [(i, i ^ 1 << bit) for i in range(n)])  78.7 us
    ppermute x30, starting transfers between devices, swap(): return lax.ppermute(x, AXES, [(i, i ^ 1 << bit) for i in range(n)])  51.3 us
    pallas_call x1, Pallas kernels, attend(): pl.pallas_call(attend_kernel, grid=(width // GROUP,), in_specs=[smem, sme...  29.8 us
    add x9, other arithmetic, body(): kept[j] = half(kept[j], my[b]) + half(got[j], my[b])  14.1 us
    dot_general x6, matrix products, outer(): lax.dot_general(rows, d, contract, preferred_element_type=jnp.float32)  9.7 us
    ppermute x6, waiting for transfers between devices, exchange(): return lax.ppermute(x, 'lang', [(i, i ^ d) for i in range(n_lang)])  8.28 us
    dot_general x3, matrix products, project(): jnp.dot(rows.reshape(-1, rows.shape[-1]), weight, preferred_element_type=...  6.35 us
    ppermute x6, starting transfers between devices, exchange(): return lax.ppermute(x, 'lang', [(i, i ^ d) for i in range(n_lang)])  6.14 us
  transfers between devices with their start and end apart: 36, of which 18 were waited for; matrix products, arithmetic and copies ran while one was open for 17% of the time, Pallas kernels for 0%

profile of v2, /device:TPU:0, one launch (start us, length us, event | category | flops | bytes accessed | tf_op | source)
XLA Modules:
  0.0 238.1 jit_solution(966158775972459150)
XLA Ops:
  15.0 3.8 %convolution_convert_fusion.2 = bf16[512,1024]{1,0:T(8,128)(2,1)} fusion(bf16[512,1024]{1,0:T(8,128)(2,1)S(1)} %bitcast.79, bf16[1024,1024]{1,0:T(8,128)(2,1)} %param.13), kind=kOutput, calls=%fused_computation.9 | convolution fusion | flops 1074266112 | bytes 4194304 | tf_op jit(solution)/shard_map/dot_general | solution.py:162
  21.4 5.8 %collective-permute-done.1 = bf16[1,128,1024]{2,1,0:T(8,128)(2,1)} collective-permute-done((bf16[1,128,1024]{2,1,0:T(8,128)(2,1)}, bf16[1,128,1024]{2,1,0:T(8,128)(2,1)}, u32[]{:S(2)}, u32[]{:S(2)}) %collective-permute-start.1) | collective-permute-done | bytes 262176 | tf_op jit(solution)/shard_map/ppermute | solution.py:197
  32.0 29.8 %shard_map.128 = (bf16[4,128,1024]{2,1,0:T(8,128)(2,1)}, bf16[4,128,1024]{2,1,0:T(8,128)(2,1)S(1)}, bf16[4,128,1024]{2,1,0:T(8,128)(2,1)S(1)}, bf16[4,128,1024]{2,1,0:T(8,128)(2,1)S(1)}) custom-call(s32[16]{0:T(128)S(1)} %bitcast.67, s32[16]{0:T(128)S(1)} %xor_bitcast_fusion.slot_ref, s32[16]{0:T(128)S(1)} %bitcast.68, bf16[4,128,1024]{2,1,0:T(8,128)(2,1)S(1)} %bitcast.69, ...), custom_call_target="tpu_custom_call" | custom-call | flops 12000000000 | bytes 30000000 | tf_op jit(solution)/shard_map/pallas_call | solution.py:139
  72.5 3.3 %dynamic-slice_add_fusion.5 = (f32[256,1024]{1,0:T(8,128)}, f32[256,1024]{1,0:T(8,128)}) fusion(f32[512,1024]{1,0:T(8,128)} %collective-permute-done.6, s32[]{:T(128)S(6)} %select_n.326, f32[512,1024]{1,0:T(8,128)S(1)} %fusion.4, s32[]{:T(128)S(6)} %select_n.329), kind=kLoop, calls=%fused_computation.19 | loop fusion | flops 524288 | bytes 6291464 | tf_op jit(solution)/shard_map/add | solution.py:245
  78.1 3.2 %dynamic-slice_add_fusion.3 = (f32[256,1024]{1,0:T(8,128)}, f32[256,1024]{1,0:T(8,128)}) fusion(f32[512,1024]{1,0:T(8,128)} %collective-permute-done.16, s32[]{:T(128)S(6)} %select_n.349, f32[512,1024]{1,0:T(8,128)S(1)} %fusion.12, s32[]{:T(128)S(6)} %select_n.351), kind=kLoop, calls=%fused_computation.17 | loop fusion | flops 524288 | bytes 6291464 | tf_op jit(solution)/shard_map/add | solution.py:245
  81.3 4.4 %collective-permute-start.17 = (f32[256,1024]{1,0:T(8,128)}, f32[256,1024]{1,0:T(8,128)}, u32[]{:S(2)}, u32[]{:S(2)}) collective-permute-start(f32[256,1024]{1,0:T(8,128)} %get-tuple-element.28), channel_id=1, source_target_pairs={{0,16},{1,17},{2,18},{3,19},{4,20},{5,21},{6,22},{7,23},{8,24},{9,... | collective-permute-start | bytes 3145736 | tf_op jit(solution)/shard_map/ppermute | solution.py:173
  85.7 3.3 %dynamic-slice_add_fusion.1 = (f32[256,1024]{1,0:T(8,128)}, f32[256,1024]{1,0:T(8,128)}) fusion(f32[512,1024]{1,0:T(8,128)} %collective-permute-done.26, s32[]{:T(128)S(6)} %select_n.371, f32[512,1024]{1,0:T(8,128)S(1)} %fusion.10, s32[]{:T(128)S(6)} %select_n.373), kind=kLoop, calls=%fused_computation.15 | loop fusion | flops 524288 | bytes 6291464 | tf_op jit(solution)/shard_map/add | solution.py:245
  97.2 5.0 %collective-permute-done.7 = f32[256,1024]{1,0:T(8,128)} collective-permute-done((f32[256,1024]{1,0:T(8,128)}, f32[256,1024]{1,0:T(8,128)}, u32[]{:S(2)}, u32[]{:S(2)}) %collective-permute-start.7) | collective-permute-done | bytes 1048608 | tf_op jit(solution)/shard_map/ppermute | solution.py:173
  103.6 6.2 %collective-permute-start.8 = (f32[128,1024]{1,0:T(8,128)S(1)}, f32[128,1024]{1,0:T(8,128)S(1)}, u32[]{:S(2)}, u32[]{:S(2)}) collective-permute-start(f32[128,1024]{1,0:T(8,128)S(1)} %get-tuple-element.42), channel_id=1, source_target_pairs={{0,16},{1,17},{2,18},{3,19},{4,20},{5,21},{6,22},{7,23},{8,24},{9,... | collective-permute-start | bytes 1572872 | tf_op jit(solution)/shard_map/ppermute | solution.py:173
  111.3 4.1 %collective-permute-start.18 = (f32[128,1024]{1,0:T(8,128)S(1)}, f32[128,1024]{1,0:T(8,128)S(1)}, u32[]{:S(2)}, u32[]{:S(2)}) collective-permute-start(f32[128,1024]{1,0:T(8,128)S(1)} %get-tuple-element.38), channel_id=1, source_target_pairs={{0,2},{1,3},{2,0},{3,1},{4,6},{5,7},{6,4},{7,5},{8,10},{9,11},{10,... | collective-permute-start | bytes 1572872 | tf_op jit(solution)/shard_map/ppermute | solution.py:173
  117.0 5.7 %collective-permute-start.28 = (f32[128,1024]{1,0:T(8,128)S(1)}, f32[128,1024]{1,0:T(8,128)S(1)}, u32[]{:S(2)}, u32[]{:S(2)}) collective-permute-start(f32[128,1024]{1,0:T(8,128)S(1)} %get-tuple-element.34), channel_id=1, source_target_pairs={{0,4},{1,5},{2,6},{3,7},{4,0},{5,1},{6,2},{7,3},{8,12},{9,13},{10,... | collective-permute-start | bytes 1572872 | tf_op jit(solution)/shard_map/ppermute | solution.py:173
  126.0 11.6 %collective-permute-done.18 = f32[128,1024]{1,0:T(8,128)S(1)} collective-permute-done((f32[128,1024]{1,0:T(8,128)S(1)}, f32[128,1024]{1,0:T(8,128)S(1)}, u32[]{:S(2)}, u32[]{:S(2)}) %collective-permute-start.18) | collective-permute-done | bytes 524320 | tf_op jit(solution)/shard_map/ppermute | solution.py:173
  137.9 7.6 %collective-permute-done.28 = f32[128,1024]{1,0:T(8,128)S(1)} collective-permute-done((f32[128,1024]{1,0:T(8,128)S(1)}, f32[128,1024]{1,0:T(8,128)S(1)}, u32[]{:S(2)}, u32[]{:S(2)}) %collective-permute-start.28) | collective-permute-done | bytes 524320 | tf_op jit(solution)/shard_map/ppermute | solution.py:173
  150.0 5.0 %collective-permute-done.19 = f32[64,1024]{1,0:T(8,128)S(1)} collective-permute-done((f32[64,1024]{1,0:T(8,128)S(1)}, f32[64,1024]{1,0:T(8,128)S(1)}, u32[]{:S(2)}, u32[]{:S(2)}) %collective-permute-start.19) | collective-permute-done | bytes 262176 | tf_op jit(solution)/shard_map/ppermute | solution.py:173
  155.7 8.6 %collective-permute-done.10 = f32[32,1024]{1,0:T(8,128)S(1)} collective-permute-done((f32[32,1024]{1,0:T(8,128)S(1)}, f32[32,1024]{1,0:T(8,128)S(1)}, u32[]{:S(2)}, u32[]{:S(2)}) %collective-permute-start.10) | collective-permute-done | bytes 131104 | tf_op jit(solution)/shard_map/ppermute | solution.py:173
  165.1 10.0 %collective-permute-done.30 = f32[32,1024]{1,0:T(8,128)S(1)} collective-permute-done((f32[32,1024]{1,0:T(8,128)S(1)}, f32[32,1024]{1,0:T(8,128)S(1)}, u32[]{:S(2)}, u32[]{:S(2)}) %collective-permute-start.30) | collective-permute-done | bytes 131104 | tf_op jit(solution)/shard_map/ppermute | solution.py:173
  179.4 4.6 %collective-permute-start.12 = (bf16[64,1024]{1,0:T(8,128)(2,1)S(1)}, bf16[64,1024]{1,0:T(8,128)(2,1)S(1)}, u32[]{:S(2)}, u32[]{:S(2)}) collective-permute-start(bf16[64,1024]{1,0:T(8,128)(2,1)S(1)} %pad_maximum_fusion.13), channel_id=1, source_target_pairs={{0,2},{1,3},{2,0},{3,1},{4,6},{5,7},{6,4},{7,5},{8,10},{9,11},{10,... | collective-permute-start | bytes 393224 | tf_op jit(solution)/shard_map/ppermute | solution.py:173
  184.0 3.4 %collective-permute-start.22 = (bf16[64,1024]{1,0:T(8,128)(2,1)S(1)}, bf16[64,1024]{1,0:T(8,128)(2,1)S(1)}, u32[]{:S(2)}, u32[]{:S(2)}) collective-permute-start(bf16[64,1024]{1,0:T(8,128)(2,1)S(1)} %pad_maximum_fusion.14), channel_id=1, source_target_pairs={{0,4},{1,5},{2,6},{3,7},{4,0},{5,1},{6,2},{7,3},{8,12},{9,13},{10,... | collective-permute-start | bytes 393224 | tf_op jit(solution)/shard_map/ppermute | solution.py:173
  189.8 4.0 %collective-permute-done.22 = bf16[64,1024]{1,0:T(8,128)(2,1)S(1)} collective-permute-done((bf16[64,1024]{1,0:T(8,128)(2,1)S(1)}, bf16[64,1024]{1,0:T(8,128)(2,1)S(1)}, u32[]{:S(2)}, u32[]{:S(2)}) %collective-permute-start.22) | collective-permute-done | bytes 131104 | tf_op jit(solution)/shard_map/ppermute | solution.py:173
  195.5 4.6 %collective-permute-done.13 = bf16[128,1024]{1,0:T(8,128)(2,1)S(1)} collective-permute-done((bf16[128,1024]{1,0:T(8,128)(2,1)S(1)}, bf16[128,1024]{1,0:T(8,128)(2,1)S(1)}, u32[]{:S(2)}, u32[]{:S(2)}) %collective-permute-start.13) | collective-permute-done | bytes 262176 | tf_op jit(solution)/shard_map/ppermute | solution.py:173
  205.7 6.9 %collective-permute-done.33 = bf16[128,1024]{1,0:T(8,128)(2,1)S(1)} collective-permute-done((bf16[128,1024]{1,0:T(8,128)(2,1)S(1)}, bf16[128,1024]{1,0:T(8,128)(2,1)S(1)}, u32[]{:S(2)}, u32[]{:S(2)}) %collective-permute-start.33) | collective-permute-done | bytes 262176 | tf_op jit(solution)/shard_map/ppermute | solution.py:173
  213.4 4.2 %collective-permute-start.34 = (bf16[256,1024]{1,0:T(8,128)(2,1)S(1)}, bf16[256,1024]{1,0:T(8,128)(2,1)S(1)}, u32[]{:S(2)}, u32[]{:S(2)}) collective-permute-start(bf16[256,1024]{1,0:T(8,128)(2,1)S(1)} %pad_maximum_fusion.9), channel_id=1, source_target_pairs={{0,2},{1,3},{2,0},{3,1},{4,6},{5,7},{6,4},{7,5},{8,10},{9,11},{10,... | collective-permute-start | bytes 1572872 | tf_op jit(solution)/shard_map/ppermute | solution.py:173
  218.0 3.8 %collective-permute-done.24 = bf16[256,1024]{1,0:T(8,128)(2,1)S(1)} collective-permute-done((bf16[256,1024]{1,0:T(8,128)(2,1)S(1)}, bf16[256,1024]{1,0:T(8,128)(2,1)S(1)}, u32[]{:S(2)}, u32[]{:S(2)}) %collective-permute-start.24) | collective-permute-done | bytes 524320 | tf_op jit(solution)/shard_map/ppermute | solution.py:173
  222.1 5.0 %collective-permute-done.34 = bf16[256,1024]{1,0:T(8,128)(2,1)S(1)} collective-permute-done((bf16[256,1024]{1,0:T(8,128)(2,1)S(1)}, bf16[256,1024]{1,0:T(8,128)(2,1)S(1)}, u32[]{:S(2)}, u32[]{:S(2)}) %collective-permute-start.34) | collective-permute-done | bytes 524320 | tf_op jit(solution)/shard_map/ppermute | solution.py:173
  (157 shorter events, 75.2 us)
Async XLA Ops:
  14.4 12.8 %collective-permute-start.1 = (bf16[1,128,1024]{2,1,0:T(8,128)(2,1)}, bf16[1,128,1024]{2,1,0:T(8,128)(2,1)}, u32[]{:S(2)}, u32[]{:S(2)}) collective-permute-start(bf16[1,128,1024]{2,1,0:T(8,128)(2,1)} %get-tuple-element.62), channel_id=1, source_target_pairs={{0,16},{8,24},{16,0},{24,8},{1,17},{9,25},{17,1},{25,9},{2,18},{10... | collective-permute-start | bytes 786440 | tf_op jit(solution)/shard_map/ppermute | solution.py:197
  15.0 12.2 %collective-permute-start = (bf16[1,128,1024]{2,1,0:T(8,128)(2,1)}, bf16[1,128,1024]{2,1,0:T(8,128)(2,1)}, u32[]{:S(2)}, u32[]{:S(2)}) collective-permute-start(bf16[1,128,1024]{2,1,0:T(8,128)(2,1)} %get-tuple-element.60), channel_id=1, source_target_pairs={{0,8},{8,0},{16,24},{24,16},{1,9},{9,1},{17,25},{25,17},{2,10},{10... | collective-permute-start | bytes 786440 | tf_op jit(solution)/shard_map/ppermute | solution.py:197
  66.0 12.1 %collective-permute-start.16 = (f32[512,1024]{1,0:T(8,128)}, f32[512,1024]{1,0:T(8,128)}, u32[]{:S(2)}, u32[]{:S(2)}) collective-permute-start(f32[512,1024]{1,0:T(8,128)} %fusion.8), channel_id=1, source_target_pairs={{0,8},{1,9},{2,10},{3,11},{4,12},{5,13},{6,14},{7,15},{8,0},{9,1},... | collective-permute-start | bytes 6291464 | tf_op jit(solution)/shard_map/ppermute | solution.py:173
  68.5 17.2 %collective-permute-start.26 = (f32[512,1024]{1,0:T(8,128)}, f32[512,1024]{1,0:T(8,128)}, u32[]{:S(2)}, u32[]{:S(2)}) collective-permute-start(f32[512,1024]{1,0:T(8,128)} %fusion.6), channel_id=1, source_target_pairs={{0,8},{1,9},{2,10},{3,11},{4,12},{5,13},{6,14},{7,15},{8,0},{9,1},... | collective-permute-start | bytes 6291464 | tf_op jit(solution)/shard_map/ppermute | solution.py:173
  75.8 26.4 %collective-permute-start.7 = (f32[256,1024]{1,0:T(8,128)}, f32[256,1024]{1,0:T(8,128)}, u32[]{:S(2)}, u32[]{:S(2)}) collective-permute-start(f32[256,1024]{1,0:T(8,128)} %get-tuple-element.30), channel_id=1, source_target_pairs={{0,1},{1,0},{2,3},{3,2},{4,5},{5,4},{6,7},{7,6},{8,9},{9,8},{10,11... | collective-permute-start | bytes 3145736 | tf_op jit(solution)/shard_map/ppermute | solution.py:173
  81.3 28.6 %collective-permute-start.17 = (f32[256,1024]{1,0:T(8,128)}, f32[256,1024]{1,0:T(8,128)}, u32[]{:S(2)}, u32[]{:S(2)}) collective-permute-start(f32[256,1024]{1,0:T(8,128)} %get-tuple-element.28), channel_id=1, source_target_pairs={{0,16},{1,17},{2,18},{3,19},{4,20},{5,21},{6,22},{7,23},{8,24},{9,... | collective-permute-start | bytes 3145736 | tf_op jit(solution)/shard_map/ppermute | solution.py:173
  89.0 26.7 %collective-permute-start.27 = (f32[256,1024]{1,0:T(8,128)}, f32[256,1024]{1,0:T(8,128)}, u32[]{:S(2)}, u32[]{:S(2)}) collective-permute-start(f32[256,1024]{1,0:T(8,128)} %get-tuple-element.26), channel_id=1, source_target_pairs={{0,2},{1,3},{2,0},{3,1},{4,6},{5,7},{6,4},{7,5},{8,10},{9,11},{10,... | collective-permute-start | bytes 3145736 | tf_op jit(solution)/shard_map/ppermute | solution.py:173
  103.6 20.4 %collective-permute-start.8 = (f32[128,1024]{1,0:T(8,128)S(1)}, f32[128,1024]{1,0:T(8,128)S(1)}, u32[]{:S(2)}, u32[]{:S(2)}) collective-permute-start(f32[128,1024]{1,0:T(8,128)S(1)} %get-tuple-element.42), channel_id=1, source_target_pairs={{0,16},{1,17},{2,18},{3,19},{4,20},{5,21},{6,22},{7,23},{8,24},{9,... | collective-permute-start | bytes 1572872 | tf_op jit(solution)/shard_map/ppermute | solution.py:173
  111.3 26.3 %collective-permute-start.18 = (f32[128,1024]{1,0:T(8,128)S(1)}, f32[128,1024]{1,0:T(8,128)S(1)}, u32[]{:S(2)}, u32[]{:S(2)}) collective-permute-start(f32[128,1024]{1,0:T(8,128)S(1)} %get-tuple-element.38), channel_id=1, source_target_pairs={{0,2},{1,3},{2,0},{3,1},{4,6},{5,7},{6,4},{7,5},{8,10},{9,11},{10,... | collective-permute-start | bytes 1572872 | tf_op jit(solution)/shard_map/ppermute | solution.py:173
  117.0 28.5 %collective-permute-start.28 = (f32[128,1024]{1,0:T(8,128)S(1)}, f32[128,1024]{1,0:T(8,128)S(1)}, u32[]{:S(2)}, u32[]{:S(2)}) collective-permute-start(f32[128,1024]{1,0:T(8,128)S(1)} %get-tuple-element.34), channel_id=1, source_target_pairs={{0,4},{1,5},{2,6},{3,7},{4,0},{5,1},{6,2},{7,3},{8,12},{9,13},{10,... | collective-permute-start | bytes 1572872 | tf_op jit(solution)/shard_map/ppermute | solution.py:173
  124.1 25.8 %collective-permute-start.9 = (f32[64,1024]{1,0:T(8,128)S(1)}, f32[64,1024]{1,0:T(8,128)S(1)}, u32[]{:S(2)}, u32[]{:S(2)}) collective-permute-start(f32[64,1024]{1,0:T(8,128)S(1)} %get-tuple-element.58), channel_id=1, source_target_pairs={{0,2},{1,3},{2,0},{3,1},{4,6},{5,7},{6,4},{7,5},{8,10},{9,11},{10,... | collective-permute-start | bytes 786440 | tf_op jit(solution)/shard_map/ppermute | solution.py:173
  137.6 17.4 %collective-permute-start.19 = (f32[64,1024]{1,0:T(8,128)S(1)}, f32[64,1024]{1,0:T(8,128)S(1)}, u32[]{:S(2)}, u32[]{:S(2)}) collective-permute-start(f32[64,1024]{1,0:T(8,128)S(1)} %get-tuple-element.54), channel_id=1, source_target_pairs={{0,4},{1,5},{2,6},{3,7},{4,0},{5,1},{6,2},{7,3},{8,12},{9,13},{10,... | collective-permute-start | bytes 786440 | tf_op jit(solution)/shard_map/ppermute | solution.py:173
  145.6 9.4 %collective-permute-start.29 = (f32[64,1024]{1,0:T(8,128)S(1)}, f32[64,1024]{1,0:T(8,128)S(1)}, u32[]{:S(2)}, u32[]{:S(2)}) collective-permute-start(f32[64,1024]{1,0:T(8,128)S(1)} %get-tuple-element.50), channel_id=1, source_target_pairs={{0,1},{1,0},{2,3},{3,2},{4,5},{5,4},{6,7},{7,6},{8,9},{9,8},{10,11... | collective-permute-start | bytes 786440 | tf_op jit(solution)/shard_map/ppermute | solution.py:173
  146.8 80.9 %collective-permute-start.5 = (f32[1,128,1024]{2,1,0:T(8,128)S(1)}, f32[1,128,1024]{2,1,0:T(8,128)S(1)}, u32[]{:S(2)}, u32[]{:S(2)}) collective-permute-start(f32[1,128,1024]{2,1,0:T(8,128)S(1)} %get-tuple-element.44), channel_id=1, source_target_pairs={{0,24},{8,16},{16,8},{24,0},{1,25},{9,17},{17,9},{25,1},{2,26},{10... | collective-permute-start | bytes 1572872 | tf_op jit(solution)/shard_map/ppermute | solution.py:197
  146.9 81.4 %collective-permute-start.4 = (f32[1,128,1024]{2,1,0:T(8,128)S(1)}, f32[1,128,1024]{2,1,0:T(8,128)S(1)}, u32[]{:S(2)}, u32[]{:S(2)}) collective-permute-start(f32[1,128,1024]{2,1,0:T(8,128)S(1)} %get-tuple-element.45), channel_id=1, source_target_pairs={{0,16},{8,24},{16,0},{24,8},{1,17},{9,25},{17,1},{25,9},{2,18},{10... | collective-permute-start | bytes 1572872 | tf_op jit(solution)/shard_map/ppermute | solution.py:197
  149.9 78.4 %collective-permute-start.3 = (f32[1,128,1024]{2,1,0:T(8,128)S(1)}, f32[1,128,1024]{2,1,0:T(8,128)S(1)}, u32[]{:S(2)}, u32[]{:S(2)}) collective-permute-start(f32[1,128,1024]{2,1,0:T(8,128)S(1)} %get-tuple-element.46), channel_id=1, source_target_pairs={{0,8},{8,0},{16,24},{24,16},{1,9},{9,1},{17,25},{25,17},{2,10},{10... | collective-permute-start | bytes 1572872 | tf_op jit(solution)/shard_map/ppermute | solution.py:197
  155.0 9.4 %collective-permute-start.10 = (f32[32,1024]{1,0:T(8,128)S(1)}, f32[32,1024]{1,0:T(8,128)S(1)}, u32[]{:S(2)}, u32[]{:S(2)}) collective-permute-start(f32[32,1024]{1,0:T(8,128)S(1)} %dynamic-slice_add_fusion.20), channel_id=1, source_target_pairs={{0,4},{1,5},{2,6},{3,7},{4,0},{5,1},{6,2},{7,3},{8,12},{9,13},{10,... | collective-permute-start | bytes 393224 | tf_op jit(solution)/shard_map/ppermute | solution.py:173
  155.0 9.9 %collective-permute-start.20 = (f32[32,1024]{1,0:T(8,128)S(1)}, f32[32,1024]{1,0:T(8,128)S(1)}, u32[]{:S(2)}, u32[]{:S(2)}) collective-permute-start(f32[32,1024]{1,0:T(8,128)S(1)} %dynamic-slice_add_fusion.19), channel_id=1, source_target_pairs={{0,1},{1,0},{2,3},{3,2},{4,5},{5,4},{6,7},{7,6},{8,9},{9,8},{10,11... | collective-permute-start | bytes 393224 | tf_op jit(solution)/shard_map/ppermute | solution.py:173
  164.4 10.8 %collective-permute-start.30 = (f32[32,1024]{1,0:T(8,128)S(1)}, f32[32,1024]{1,0:T(8,128)S(1)}, u32[]{:S(2)}, u32[]{:S(2)}) collective-permute-start(f32[32,1024]{1,0:T(8,128)S(1)} %dynamic-slice_add_fusion.18), channel_id=1, source_target_pairs={{0,16},{1,17},{2,18},{3,19},{4,20},{5,21},{6,22},{7,23},{8,24},{9,... | collective-permute-start | bytes 393224 | tf_op jit(solution)/shard_map/ppermute | solution.py:173
  165.0 11.3 %collective-permute-start.11 = (bf16[32,1024]{1,0:T(8,128)(2,1)S(1)}, bf16[32,1024]{1,0:T(8,128)(2,1)S(1)}, u32[]{:S(2)}, u32[]{:S(2)}) collective-permute-start(bf16[32,1024]{1,0:T(8,128)(2,1)S(1)} %multiply_convert_fusion.2), channel_id=1, source_target_pairs={{0,4},{1,5},{2,6},{3,7},{4,0},{5,1},{6,2},{7,3},{8,12},{9,13},{10,... | collective-permute-start | bytes 196616 | tf_op jit(solution)/shard_map/ppermute | solution.py:173
  184.0 9.8 %collective-permute-start.22 = (bf16[64,1024]{1,0:T(8,128)(2,1)S(1)}, bf16[64,1024]{1,0:T(8,128)(2,1)S(1)}, u32[]{:S(2)}, u32[]{:S(2)}) collective-permute-start(bf16[64,1024]{1,0:T(8,128)(2,1)S(1)} %pad_maximum_fusion.14), channel_id=1, source_target_pairs={{0,4},{1,5},{2,6},{3,7},{4,0},{5,1},{6,2},{7,3},{8,12},{9,13},{10,... | collective-permute-start | bytes 393224 | tf_op jit(solution)/shard_map/ppermute | solution.py:173
  200.2 12.4 %collective-permute-start.33 = (bf16[128,1024]{1,0:T(8,128)(2,1)S(1)}, bf16[128,1024]{1,0:T(8,128)(2,1)S(1)}, u32[]{:S(2)}, u32[]{:S(2)}) collective-permute-start(bf16[128,1024]{1,0:T(8,128)(2,1)S(1)} %pad_maximum_fusion.12), channel_id=1, source_target_pairs={{0,4},{1,5},{2,6},{3,7},{4,0},{5,1},{6,2},{7,3},{8,12},{9,13},{10,... | collective-permute-start | bytes 786440 | tf_op jit(solution)/shard_map/ppermute | solution.py:173
  203.9 9.6 %collective-permute-start.14 = (bf16[256,1024]{1,0:T(8,128)(2,1)S(1)}, bf16[256,1024]{1,0:T(8,128)(2,1)S(1)}, u32[]{:S(2)}, u32[]{:S(2)}) collective-permute-start(bf16[256,1024]{1,0:T(8,128)(2,1)S(1)} %pad_maximum_fusion.7), channel_id=1, source_target_pairs={{0,1},{1,0},{2,3},{3,2},{4,5},{5,4},{6,7},{7,6},{8,9},{9,8},{10,11... | collective-permute-start | bytes 1572872 | tf_op jit(solution)/shard_map/ppermute | solution.py:173
  213.4 13.7 %collective-permute-start.34 = (bf16[256,1024]{1,0:T(8,128)(2,1)S(1)}, bf16[256,1024]{1,0:T(8,128)(2,1)S(1)}, u32[]{:S(2)}, u32[]{:S(2)}) collective-permute-start(bf16[256,1024]{1,0:T(8,128)(2,1)S(1)} %pad_maximum_fusion.9), channel_id=1, source_target_pairs={{0,2},{1,3},{2,0},{3,1},{4,6},{5,7},{6,4},{7,5},{8,10},{9,11},{10,... | collective-permute-start | bytes 1572872 | tf_op jit(solution)/shard_map/ppermute | solution.py:173
  (34 other events, 289.6 us)

commit v3 on v2

--- a/solution.py
+++ b/solution.py
@@ -1,3 +1,5 @@
+import functools
+
 import jax
 import jax.numpy as jnp
 from jax import lax
@@ -178,6 +180,152 @@
     return lax.dynamic_slice_in_dim(x, which * rows, rows, axis)
 
 
+def flip(x, d):
+    b = 0
+    out = x
+    while (1 << b) <= d:
+        if (d >> b) & 1:
+            out = out + (1 - 2 * ((x // (1 << b)) % 2)) * (1 << b)
+        b += 1
+    return out
+
+
+def reduce_kernel(
+    n_lang, n_pair, orders, factor,
+    kept0, kept1, kept2, got0, got1, got2, dxt,
+    whole0, whole1, whole2, ret,
+    kbuf, rbuf, sbuf,
+    rs_send, rs_recv, ag_send, ag_recv, fw_send, fw_recv, ret_send, ret_recv,
+):
+    lang, pair = lax.axis_index("lang"), lax.axis_index("pair")
+    pair_bits = n_pair.bit_length() - 1
+    mesh_id = pl.DeviceIdType.MESH
+    kept, got, whole = (kept0, kept1, kept2), (got0, got1, got2), (whole0, whole1, whole2)
+    height, cols = kept0.shape
+    steps = len(orders[0])
+
+    def across(b):
+        if b < pair_bits:
+            return (lang, flip(pair, 1 << b))
+        return (flip(lang, 1 << (b - pair_bits)), pair)
+
+    def mine(b):
+        if b < pair_bits:
+            return (pair // (1 << b)) % 2
+        return (lang // (1 << (b - pair_bits))) % 2
+
+    core = pair_bits
+    col = pl.multiple_of(mine(core) * cols, cols)
+
+    partners = [across(b) for b in range(pair_bits)] + [
+        (flip(lang, d), pair) for d in range(1, n_lang)]
+    barrier = pltpu.get_barrier_semaphore()
+    for p in partners:
+        pl.semaphore_signal(barrier, inc=1, device_id=p, device_id_type=mesh_id)
+    pl.semaphore_wait(barrier, len(partners))
+
+    started = []
+
+    def send(src, dst, send_sem, recv_sem, device):
+        copy = pltpu.make_async_remote_copy(
+            src_ref=src, dst_ref=dst, send_sem=send_sem, recv_sem=recv_sem,
+            device_id=device, device_id_type=mesh_id)
+        copy.start()
+        started.append(copy)
+        return copy
+
+    pending = [None, None, None]
+    for step in range(steps):
+        rows = height >> (step + 1)
+        at = pl.ds(height - (height >> step), rows)
+        before = height - 2 * (height >> step)
+        for j in range(3):
+            b = orders[j][step]
+            if step:
+                pending[j].wait_recv()
+
+            def both(which):
+                if step == 0:
+                    part = pl.ds(pl.multiple_of(which * rows, rows), rows)
+                    return kept[j][part] + got[j][part]
+                part = pl.ds(pl.multiple_of(before + which * rows, rows), rows)
+                return kbuf[j, part] + rbuf[j, part]
+
+            sbuf[j, at] = both(1 - mine(b))
+            pending[j] = send(sbuf.at[j, at], rbuf.at[j, at], rs_send.at[j, step],
+                              rs_recv.at[j, step], across(b))
+            kbuf[j, at] = both(mine(b))
+        if step == 0:
+            returns = [
+                send(dxt.at[d], ret.at[d - 1], ret_send.at[d - 1], ret_recv.at[d - 1],
+                     (flip(lang, d), pair))
+                for d in range(1, n_lang)]
+
+    arrived = []
+
+    def forward(j, n, row, rows):
+        part = whole[j].at[pl.ds(row, rows), pl.ds(col, cols)]
+        arrived.append(send(part, part, fw_send.at[j, n], fw_recv.at[j, n], across(core)))
+
+    offsets = []
+    for j in range(3):
+        row, offs = 0, []
+        for step in range(steps):
+            rows = height >> (step + 1)
+            row = row + mine(orders[j][step]) * rows
+            offs.append(row)
+        offsets.append(offs)
+
+    last = height >> steps
+    for step in reversed(range(steps)):
+        rows = height >> (step + 1)
+        for j in range(3):
+            b = orders[j][step]
+            row = pl.multiple_of(offsets[j][step], rows)
+            pending[j].wait_recv()
+            if step == steps - 1:
+                at = pl.ds(height - (height >> step), last)
+                total = kbuf[j, at] + rbuf[j, at]
+                whole[j][pl.ds(row, last), pl.ds(col, cols)] = (total * factor).astype(jnp.bfloat16)
+            part = whole[j].at[pl.ds(row, rows), pl.ds(col, cols)]
+            pending[j] = send(part, part, ag_send.at[j, step], ag_recv.at[j, step], across(b))
+            if step == steps - 1:
+                forward(j, steps, row, rows)
+            else:
+                up = orders[j][step + 1]
+                small = height >> (step + 2)
+                other = offsets[j][step + 1] + (1 - 2 * mine(up)) * small
+                forward(j, step + 1, pl.multiple_of(other, small), small)
+    for j in range(3):
+        pending[j].wait_recv()
+        b, rows = orders[j][0], height >> 1
+        forward(j, 0, pl.multiple_of((1 - mine(b)) * rows, rows), rows)
+    for copy in returns + arrived:
+        copy.wait_recv()
+    for copy in started:
+        copy.wait_send()
+
+
+def reduce_all(n_lang, n_pair, orders, factor, kept, got, dxt):
+    height, cols = kept[0].shape
+    steps = len(orders[0])
+    vmem = pl.BlockSpec(memory_space=pltpu.VMEM)
+    sem = pltpu.SemaphoreType.DMA
+    made = jax.ShapeDtypeStruct((height, 2 * cols), jnp.bfloat16)
+    return pl.pallas_call(
+        functools.partial(reduce_kernel, n_lang, n_pair, orders, factor),
+        in_specs=[vmem] * 7,
+        out_specs=[vmem] * 4,
+        out_shape=[made, made, made,
+                   jax.ShapeDtypeStruct((n_lang - 1,) + dxt.shape[1:], dxt.dtype)],
+        scratch_shapes=[pltpu.VMEM((3, height, cols), jnp.float32)] * 3 + [
+            sem((3, steps)), sem((3, steps)), sem((3, steps)), sem((3, steps)),
+            sem((3, steps + 1)), sem((3, steps + 1)), sem((n_lang - 1,)), sem((n_lang - 1,))],
+        compiler_params=pltpu.CompilerParams(
+            collective_id=0, has_side_effects=True, vmem_limit_bytes=50 * 1024 * 1024),
+    )(*kept, *got, dxt)
+
+
 def body(sentences, cotangent, w_query, w_key, w_value, send_rows, pair_src, pair_slot, pair_valid):
     sent_dev, length, width = sentences.shape
     n_lang = lax.axis_size("lang")
@@ -226,33 +374,16 @@
         (recv_flat, dk_b, upper + high + low),
         (own_flat, dq_b, low + upper + high),
     ]
-    got = [swap(outer(half(rows, 1 - my[core], 1), d), core) for rows, d, _ in jobs]
-    kept = [outer(half(rows, my[core], 1), d) for rows, d, _ in jobs]
-
+    got = [swap(outer(rows, half(d, 1 - my[core], 1)), core) for rows, d, _ in jobs]
+    kept = [outer(rows, half(d, my[core], 1)) for rows, d, _ in jobs]
     dxt = jnp.dot(dk_b, w_key.T, preferred_element_type=jnp.float32) + jnp.dot(
         dv_b, w_value.T, preferred_element_type=jnp.float32
     )
     dxt = dxt.reshape(n_lang, cap, length, width)
-    returned = [exchange(dxt[d], d) if d else dxt[d] for d in range(n_lang)]
-
-    for step in range(len(jobs[0][2])):
-        sent = []
-        for j, (_, _, order) in enumerate(jobs):
-            b = order[step]
-            sent.append(swap(half(kept[j], 1 - my[b]) + half(got[j], 1 - my[b]), b))
-        for j, (_, _, order) in enumerate(jobs):
-            b = order[step]
-            kept[j] = half(kept[j], my[b]) + half(got[j], my[b])
-        got = sent
     factor = 1.0 / (sent_dev * n_lang * n_pair * length) ** 0.5
-    whole = [((kept[j] + got[j]) * factor).astype(jnp.bfloat16) for j in range(3)]
-    for step in reversed(range(-1, len(jobs[0][2]))):
-        order = [core if step < 0 else job[2][step] for job in jobs]
-        other = [swap(whole[j], order[j]) for j in range(3)]
-        for j in range(3):
-            first = my[order[j]] == 0
-            whole[j] = jnp.concatenate([
-                jnp.where(first, whole[j], other[j]), jnp.where(first, other[j], whole[j])], axis=0)
+    grad_wv, grad_wk, grad_wq, ret = reduce_all(
+        n_lang, n_pair, [order for _, _, order in jobs], factor, kept, got, dxt)
+    returned = [dxt[0]] + [ret[d] for d in range(n_lang - 1)]
 
     grad_total = jnp.dot(dq_b, w_query.T, preferred_element_type=jnp.float32).reshape(
         sent_dev, length, width
@@ -262,7 +393,7 @@
         for c in range(cap):
             pick = (owner == listed[d][c])[:, None, None]
             grad_total = grad_total + jnp.where(pick, returned[d][c][None], 0.0)
-    return (attended, grad_total.astype(jnp.bfloat16), whole[2], whole[1], whole[0])
+    return (attended, grad_total.astype(jnp.bfloat16), grad_wq, grad_wk, grad_wv)
 
 
 def solution(mesh):

time: 239 us -> 221 us (0.925)
  Pallas kernels: 29.8 us -> 158 us
  waiting for transfers between devices: 87 us -> 8.3 us
  starting transfers between devices: 57.4 us -> 3.62 us
  other arithmetic: 28.4 us -> 5.9 us
  local copies, waits for them, and re-layouts: 4.03 us -> 9.18 us
  matrix products: 22.7 us -> 25.5 us
    pallas_call x0 -> x1, Pallas kernels: none -> 128 us  [reduce_all(): pl.pallas_call(functools.partial(reduce_kernel, n_lang, n_pair, orders, f...]
    ppermute x30 -> x3, waiting for transfers between devices: 78.7 us -> 0.01 us  [swap(): return lax.ppermute(x, AXES, [(i, i ^ 1 << bit) for i in range(n)])]
    ppermute x30 -> x3, starting transfers between devices: 51.3 us -> 0.51 us  [swap(): return lax.ppermute(x, AXES, [(i, i ^ 1 << bit) for i in range(n)])]
    add x12 -> x0, other arithmetic: 14.1 us -> none  [the longest x9 14.1 us: body(): kept[j] = half(kept[j], my[b]) + half(got[j], my[b])]
    unnamed x44 -> x45, local copies, waits for them, and re-layouts: 2.27 us -> 7.44 us
    concatenate x15 -> x0, other arithmetic: 5.08 us -> none  [body(): jnp.concatenate([jnp.where(first, whole[j], other[j]), jnp.where(first, o...]
    select_n x15 -> x0, other arithmetic: 3.1 us -> none  [body(): jnp.where(first, whole[j], other[j])]
    ppermute x6 -> x3, starting transfers between devices: 6.14 us -> 3.11 us  [exchange(): return lax.ppermute(x, 'lang', [(i, i ^ d) for i in range(n_lang)])]
  transfers between devices with their start and end apart: 36 -> 6, of which waited for: 18 -> 2; matrix products, arithmetic and copies ran while one was open for 17% -> 10% of each run, Pallas kernels for 0% -> 0%
where the time goes in v3:
time: 221 us; the launch traced here: 219 us
  Pallas kernels  158 us (71%)
  matrix products  25.5 us (12%)
  local copies, waits for them, and re-layouts  9.18 us (4%)
  between operations  8.58 us (4%)
  waiting for transfers between devices  8.3 us (4%)
  other arithmetic  5.9 us (3%)
  starting transfers between devices  3.62 us (2%)
    pallas_call x1, Pallas kernels, reduce_all(): pl.pallas_call(functools.partial(reduce_kernel, n_lang, n_pair, orders, f...  128 us
    pallas_call x1, Pallas kernels, attend(): pl.pallas_call(attend_kernel, grid=(width // GROUP,), in_specs=[smem, sme...  29.8 us
    dot_general x6, matrix products, outer(): lax.dot_general(rows, d, contract, preferred_element_type=jnp.float32)  12.6 us
    ppermute x3, waiting for transfers between devices, exchange(): return lax.ppermute(x, 'lang', [(i, i ^ d) for i in range(n_lang)])  8.29 us
    unnamed x45, local copies, waits for them, and re-layouts  7.44 us
    dot_general x3, matrix products, project(): jnp.dot(rows.reshape(-1, rows.shape[-1]), weight, preferred_element_type=...  6.36 us
  transfers between devices with their start and end apart: 6, of which 2 were waited for; matrix products, arithmetic and copies ran while one was open for 10% of the time, Pallas kernels for 0%

profile of v3, /device:TPU:0, one launch (start us, length us, event | category | flops | bytes accessed | tf_op | source)
XLA Modules:
  0.0 218.7 jit_solution(14878626324338794269)
XLA Ops:
  0.7 1.5 constant_dynamic-slice_fusion.3
  9.9 2.1 dynamic-slice_select_fusion.3
  12.0 2.4 %collective-permute-start.2 = (bf16[1,128,1024]{2,1,0:T(8,128)(2,1)}, bf16[1,128,1024]{2,1,0:T(8,128)(2,1)}, u32[]{:S(2)}, u32[]{:S(2)}) collective-permute-start(bf16[1,128,1024]{2,1,0:T(8,128)(2,1)} %get-tuple-element.38), channel_id=1, source_target_pairs={{0,24},{8,16},{16,8},{24,0},{1,25},{9,17},{17,9},{25,1},{2,26},{10... | collective-permute-start | bytes 786440 | tf_op jit(solution)/shard_map/ppermute | solution.py:345
  15.1 3.8 %convolution_convert_fusion.2 = bf16[512,1024]{1,0:T(8,128)(2,1)} fusion(bf16[512,1024]{1,0:T(8,128)(2,1)S(1)} %bitcast.80, bf16[1024,1024]{1,0:T(8,128)(2,1)} %param.13), kind=kOutput, calls=%fused_computation.8 | convolution fusion | flops 1074266112 | bytes 4194304 | tf_op jit(solution)/shard_map/dot_general | solution.py:164
  18.9 2.5 %collective-permute-done.2 = bf16[1,128,1024]{2,1,0:T(8,128)(2,1)} collective-permute-done((bf16[1,128,1024]{2,1,0:T(8,128)(2,1)}, bf16[1,128,1024]{2,1,0:T(8,128)(2,1)}, u32[]{:S(2)}, u32[]{:S(2)}) %collective-permute-start.2) | collective-permute-done | bytes 262176 | tf_op jit(solution)/shard_map/ppermute | solution.py:345
  21.4 5.8 %collective-permute-done.1 = bf16[1,128,1024]{2,1,0:T(8,128)(2,1)} collective-permute-done((bf16[1,128,1024]{2,1,0:T(8,128)(2,1)}, bf16[1,128,1024]{2,1,0:T(8,128)(2,1)}, u32[]{:S(2)}, u32[]{:S(2)}) %collective-permute-start.1) | collective-permute-done | bytes 262176 | tf_op jit(solution)/shard_map/ppermute | solution.py:345
  28.5 1.3 convolution_convert_fusion.1
  30.5 1.3 convolution_convert_fusion
  32.0 29.8 %shard_map.128 = (bf16[4,128,1024]{2,1,0:T(8,128)(2,1)}, bf16[4,128,1024]{2,1,0:T(8,128)(2,1)S(1)}, bf16[4,128,1024]{2,1,0:T(8,128)(2,1)S(1)}, bf16[4,128,1024]{2,1,0:T(8,128)(2,1)S(1)}) custom-call(s32[16]{0:T(128)S(1)} %bitcast.69, s32[16]{0:T(128)S(1)} %xor_bitcast_fusion.slot_ref, s32[16]{0:T(128)S(1)} %bitcast.70, bf16[4,128,1024]{2,1,0:T(8,128)(2,1)S(1)} %bitcast.71, ...), custom_call_target="tpu_custom_call" | custom-call | flops 12000000000 | bytes 30000000 | tf_op jit(solution)/shard_map/pallas_call | solution.py:141
  61.8 2.2 fusion.5
  64.0 2.1 fusion.3
  66.6 2.1 convolution_bitcast_fusion
  70.0 1.3 iota_compare_fusion.2
  71.3 2.7 %fusion.18 = f32[512,1024]{1,0:T(8,128)S(1)} fusion(bf16[512,1024]{1,0:T(8,128)(2,1)} %bitcast.64, bf16[1024,1024]{1,0:T(8,128)(2,1)S(1)} %copy-done), kind=kOutput, calls=%fused_computation.42 | convolution fusion | flops 1073741824 | bytes 5242880 | tf_op jit(solution)/shard_map/dot_general | solution.py:379
  74.0 1.3 convolution_add_fusion
  75.4 2.1 fusion.10.kept0
  77.5 2.1 fusion.8.kept1
  79.6 2.1 convolution_bitcast_fusion.1.kept2
  81.7 127.8 %shard_map.129 = (bf16[1024,1024]{1,0:T(8,128)(2,1)S(1)}, bf16[1024,1024]{1,0:T(8,128)(2,1)}, bf16[1024,1024]{1,0:T(8,128)(2,1)}, f32[3,1,128,1024]{3,2,1,0:T(8,128)S(1)}) custom-call(f32[1024,512]{1,0:T(8,128)} %fusion.10.kept0, f32[1024,512]{1,0:T(8,128)} %fusion.8.kept1, f32[1024,512]{1,0:T(8,128)} %convolution_bitcast_fusion.1.kept2, ...), custom_call_target="tpu_custom_call" | custom-call | tf_op jit(solution)/shard_map/pallas_call | solution.py:315
  209.7 1.4 copy-done.19
  211.1 2.7 %add_convert_fusion = bf16[4,128,1024]{2,1,0:T(8,128)(2,1)} fusion(f32[128,1024]{1,0:T(8,128)S(1)} %get-tuple-element.34, f32[128,1024]{1,0:T(8,128)S(1)} %get-tuple-element.35, f32[128,1024]{1,0:T(8,128)S(1)} %get-tuple-element.33, f32[128,1024]{1,0:T(8,128)S(1)} %slice.26, pred[4]{0:T(512)(128)(4,1)S(1)} %get-tuple-element.44, ...), kind=kOutput, calls=%fused_computation.2 | convolution fusion | flops 1078460416 | bytes 6291472 | tf_op jit(solution)/shard_map/dot_general | solution.py:388
  213.7 1.3 copy.21
  216.1 1.3 copy.22
  217.4 1.3 copy.23
  (55 shorter events, 5.9 us)
Async XLA Ops:
  0.6 27.9 %copy-start = (bf16[1024,1024]{1,0:T(8,128)(2,1)S(1)}, bf16[1024,1024]{1,0:T(8,128)(2,1)}, u32[]{:S(2)}) copy-start(bf16[1024,1024]{1,0:T(8,128)(2,1)} %param.14) | copy-start | bytes 6291460
  0.6 14.5 %copy-start.11 = (bf16[4,128,1024]{2,1,0:T(8,128)(2,1)S(1)}, bf16[4,128,1024]{2,1,0:T(8,128)(2,1)}, u32[]{:S(2)}) copy-start(bf16[4,128,1024]{2,1,0:T(8,128)(2,1)} %param.11) | copy-start | bytes 3145732
  12.0 9.5 %collective-permute-start.2 = (bf16[1,128,1024]{2,1,0:T(8,128)(2,1)}, bf16[1,128,1024]{2,1,0:T(8,128)(2,1)}, u32[]{:S(2)}, u32[]{:S(2)}) collective-permute-start(bf16[1,128,1024]{2,1,0:T(8,128)(2,1)} %get-tuple-element.38), channel_id=1, source_target_pairs={{0,24},{8,16},{16,8},{24,0},{1,25},{9,17},{17,9},{25,1},{2,26},{10... | collective-permute-start | bytes 786440 | tf_op jit(solution)/shard_map/ppermute | solution.py:345
  14.4 12.8 %collective-permute-start.1 = (bf16[1,128,1024]{2,1,0:T(8,128)(2,1)}, bf16[1,128,1024]{2,1,0:T(8,128)(2,1)}, u32[]{:S(2)}, u32[]{:S(2)}) collective-permute-start(bf16[1,128,1024]{2,1,0:T(8,128)(2,1)} %get-tuple-element.39), channel_id=1, source_target_pairs={{0,16},{8,24},{16,0},{24,8},{1,17},{9,25},{17,1},{25,9},{2,18},{10... | collective-permute-start | bytes 786440 | tf_op jit(solution)/shard_map/ppermute | solution.py:345
  15.0 12.2 %collective-permute-start = (bf16[1,128,1024]{2,1,0:T(8,128)(2,1)}, bf16[1,128,1024]{2,1,0:T(8,128)(2,1)}, u32[]{:S(2)}, u32[]{:S(2)}) collective-permute-start(bf16[1,128,1024]{2,1,0:T(8,128)(2,1)} %get-tuple-element.37), channel_id=1, source_target_pairs={{0,8},{8,0},{16,24},{24,16},{1,9},{9,1},{17,25},{25,17},{2,10},{10... | collective-permute-start | bytes 786440 | tf_op jit(solution)/shard_map/ppermute | solution.py:345
  15.1 3.8 %copy-start.20 = (s32[1,16]{1,0:T(1,128)S(1)}, s32[1,16]{1,0:T(1,128)}, u32[]{:S(2)}) copy-start(s32[1,16]{1,0:T(1,128)} %param.18) | copy-start | bytes 196
  28.5 35.5 %copy-start.9 = (bf16[4,128,1024]{2,1,0:T(8,128)(2,1)}, bf16[4,128,1024]{2,1,0:T(8,128)(2,1)S(1)}, u32[]{:S(2)}) copy-start(bf16[4,128,1024]{2,1,0:T(8,128)(2,1)S(1)} %pad_maximum_fusion) | copy-start | bytes 3145732
  28.5 2.0 copy-start.17
  30.5 1.6 copy-start.8
  61.8 2.2 copy-start.3
  61.8 2.2 copy-start.1
  64.0 17.7 %collective-permute-start.3 = (f32[1024,512]{1,0:T(8,128)}, f32[1024,512]{1,0:T(8,128)}, u32[]{:S(2)}, u32[]{:S(2)}) collective-permute-start(f32[1024,512]{1,0:T(8,128)} %fusion.5), channel_id=1, source_target_pairs={{0,8},{1,9},{2,10},{3,11},{4,12},{5,13},{6,14},{7,15},{8,0},{9,1},... | collective-permute-start | bytes 6291464 | tf_op jit(solution)/shard_map/ppermute | solution.py:175
  64.0 2.6 %copy-start.12 = (bf16[4,128,1024]{2,1,0:T(8,128)(2,1)S(1)}, bf16[4,128,1024]{2,1,0:T(8,128)(2,1)}, u32[]{:S(2)}) copy-start(bf16[4,128,1024]{2,1,0:T(8,128)(2,1)} %param.11) | copy-start | bytes 3145732
  66.2 15.5 %collective-permute-start.4 = (f32[1024,512]{1,0:T(8,128)}, f32[1024,512]{1,0:T(8,128)}, u32[]{:S(2)}, u32[]{:S(2)}) collective-permute-start(f32[1024,512]{1,0:T(8,128)} %fusion.3), channel_id=1, source_target_pairs={{0,8},{1,9},{2,10},{3,11},{4,12},{5,13},{6,14},{7,15},{8,0},{9,1},... | collective-permute-start | bytes 6291464 | tf_op jit(solution)/shard_map/ppermute | solution.py:175
  68.7 12.9 %collective-permute-start.5 = (f32[1024,512]{1,0:T(8,128)}, f32[1024,512]{1,0:T(8,128)}, u32[]{:S(2)}, u32[]{:S(2)}) collective-permute-start(f32[1024,512]{1,0:T(8,128)} %convolution_bitcast_fusion), channel_id=1, source_target_pairs={{0,8},{1,9},{2,10},{3,11},{4,12},{5,13},{6,14},{7,15},{8,0},{9,1},... | collective-permute-start | bytes 6291464 | tf_op jit(solution)/shard_map/ppermute | solution.py:175
  71.3 2.7 %copy-start.4 = (bf16[4,128,1024]{2,1,0:T(8,128)(2,1)S(1)}, bf16[4,128,1024]{2,1,0:T(8,128)(2,1)}, u32[]{:S(2)}) copy-start(bf16[4,128,1024]{2,1,0:T(8,128)(2,1)} %copy-done.3) | copy-start | bytes 3145732
  71.3 2.7 %copy-start.18 = (bf16[1024,1024]{1,0:T(8,128)(2,1)S(1)}, bf16[1024,1024]{1,0:T(8,128)(2,1)}, u32[]{:S(2)}) copy-start(bf16[1024,1024]{1,0:T(8,128)(2,1)} %param.15) | copy-start | bytes 6291460
  74.0 1.4 copy-start.10
  75.3 2.2 copy-start.14
  75.4 2.1 copy-start.2
  77.5 2.1 copy-start.13
  209.5 1.6 copy-start.19
  211.1 2.7 %copy-start.16 = (bf16[1024,1024]{1,0:T(8,128)(2,1)S(1)}, bf16[1024,1024]{1,0:T(8,128)(2,1)}, u32[]{:S(2)}) copy-start(bf16[1024,1024]{1,0:T(8,128)(2,1)} %get-tuple-element.55) | copy-start | bytes 6291460
  213.7 2.3 %copy-start.15 = (bf16[1024,1024]{1,0:T(8,128)(2,1)S(1)}, bf16[1024,1024]{1,0:T(8,128)(2,1)}, u32[]{:S(2)}) copy-start(bf16[1024,1024]{1,0:T(8,128)(2,1)} %get-tuple-element.56) | copy-start | bytes 6291460
  (3 other events, 3.9 us)

commit v4 on v3

--- a/solution.py
+++ b/solution.py
@@ -194,14 +194,17 @@
     n_lang, n_pair, orders, factor,
     kept0, kept1, kept2, got0, got1, got2, dxt,
     whole0, whole1, whole2, ret,
-    kbuf, rbuf, sbuf,
+    kbuf, rbuf, sbuf, sbuf_b, rbuf_b,
     rs_send, rs_recv, ag_send, ag_recv, fw_send, fw_recv, ret_send, ret_recv,
 ):
     lang, pair = lax.axis_index("lang"), lax.axis_index("pair")
     pair_bits = n_pair.bit_length() - 1
     mesh_id = pl.DeviceIdType.MESH
     kept, got, whole = (kept0, kept1, kept2), (got0, got1, got2), (whole0, whole1, whole2)
-    height, cols = kept0.shape
+    height, job_cols = kept0.shape
+    n = len(orders)
+    per = n // 3
+    cols = job_cols // per
     steps = len(orders[0])
 
     def across(b):
@@ -215,7 +218,8 @@
         return (lang // (1 << (b - pair_bits))) % 2
 
     core = pair_bits
-    col = pl.multiple_of(mine(core) * cols, cols)
+    col = [pl.multiple_of(mine(core) * job_cols + (j % per) * cols, cols) for j in range(n)]
+    sub = [slice((j % per) * cols, (j % per + 1) * cols) for j in range(n)]
 
     partners = [across(b) for b in range(pair_bits)] + [
         (flip(lang, d), pair) for d in range(1, n_lang)]
@@ -234,12 +238,12 @@
         started.append(copy)
         return copy
 
-    pending = [None, None, None]
+    pending = [None] * n
     for step in range(steps):
         rows = height >> (step + 1)
         at = pl.ds(height - (height >> step), rows)
         before = height - 2 * (height >> step)
-        for j in range(3):
+        for j in range(n):
             b = orders[j][step]
             if step:
                 pending[j].wait_recv()
@@ -247,15 +251,22 @@
             def both(which):
                 if step == 0:
                     part = pl.ds(pl.multiple_of(which * rows, rows), rows)
-                    return kept[j][part] + got[j][part]
+                    return kept[j // per][part, sub[j]] + got[j // per][part, sub[j]]
                 part = pl.ds(pl.multiple_of(before + which * rows, rows), rows)
+                if step == 1:
+                    here = pl.ds(pl.multiple_of(which * rows, rows), rows)
+                    return kbuf[j, part] + rbuf_b[j, here].astype(jnp.float32)
                 return kbuf[j, part] + rbuf[j, part]
 
-            sbuf[j, at] = both(1 - mine(b))
-            pending[j] = send(sbuf.at[j, at], rbuf.at[j, at], rs_send.at[j, step],
-                              rs_recv.at[j, step], across(b))
+            if step == 0:
+                sbuf_b[j] = both(1 - mine(b)).astype(jnp.bfloat16)
+                source, target = sbuf_b.at[j], rbuf_b.at[j]
+            else:
+                sbuf[j, at] = both(1 - mine(b))
+                source, target = sbuf.at[j, at], rbuf.at[j, at]
+            pending[j] = send(source, target, rs_send.at[j, step], rs_recv.at[j, step], across(b))
             kbuf[j, at] = both(mine(b))
-        if step == 0:
+        if step == 1:
             returns = [
                 send(dxt.at[d], ret.at[d - 1], ret_send.at[d - 1], ret_recv.at[d - 1],
                      (flip(lang, d), pair))
@@ -263,12 +274,12 @@
 
     arrived = []
 
-    def forward(j, n, row, rows):
-        part = whole[j].at[pl.ds(row, rows), pl.ds(col, cols)]
-        arrived.append(send(part, part, fw_send.at[j, n], fw_recv.at[j, n], across(core)))
+    def forward(j, at, row, rows):
+        part = whole[j // per].at[pl.ds(row, rows), pl.ds(col[j], cols)]
+        arrived.append(send(part, part, fw_send.at[j, at], fw_recv.at[j, at], across(core)))
 
     offsets = []
-    for j in range(3):
+    for j in range(n):
         row, offs = 0, []
         for step in range(steps):
             rows = height >> (step + 1)
@@ -279,15 +290,16 @@
     last = height >> steps
     for step in reversed(range(steps)):
         rows = height >> (step + 1)
-        for j in range(3):
+        for j in range(n):
             b = orders[j][step]
             row = pl.multiple_of(offsets[j][step], rows)
             pending[j].wait_recv()
             if step == steps - 1:
                 at = pl.ds(height - (height >> step), last)
                 total = kbuf[j, at] + rbuf[j, at]
-                whole[j][pl.ds(row, last), pl.ds(col, cols)] = (total * factor).astype(jnp.bfloat16)
-            part = whole[j].at[pl.ds(row, rows), pl.ds(col, cols)]
+                whole[j // per][pl.ds(row, last), pl.ds(col[j], cols)] = (
+                    total * factor).astype(jnp.bfloat16)
+            part = whole[j // per].at[pl.ds(row, rows), pl.ds(col[j], cols)]
             pending[j] = send(part, part, ag_send.at[j, step], ag_recv.at[j, step], across(b))
             if step == steps - 1:
                 forward(j, steps, row, rows)
@@ -296,7 +308,7 @@
                 small = height >> (step + 2)
                 other = offsets[j][step + 1] + (1 - 2 * mine(up)) * small
                 forward(j, step + 1, pl.multiple_of(other, small), small)
-    for j in range(3):
+    for j in range(n):
         pending[j].wait_recv()
         b, rows = orders[j][0], height >> 1
         forward(j, 0, pl.multiple_of((1 - mine(b)) * rows, rows), rows)
@@ -308,7 +320,7 @@
 
 def reduce_all(n_lang, n_pair, orders, factor, kept, got, dxt):
     height, cols = kept[0].shape
-    steps = len(orders[0])
+    steps, n = len(orders[0]), len(orders)
     vmem = pl.BlockSpec(memory_space=pltpu.VMEM)
     sem = pltpu.SemaphoreType.DMA
     made = jax.ShapeDtypeStruct((height, 2 * cols), jnp.bfloat16)
@@ -318,9 +330,10 @@
         out_specs=[vmem] * 4,
         out_shape=[made, made, made,
                    jax.ShapeDtypeStruct((n_lang - 1,) + dxt.shape[1:], dxt.dtype)],
-        scratch_shapes=[pltpu.VMEM((3, height, cols), jnp.float32)] * 3 + [
-            sem((3, steps)), sem((3, steps)), sem((3, steps)), sem((3, steps)),
-            sem((3, steps + 1)), sem((3, steps + 1)), sem((n_lang - 1,)), sem((n_lang - 1,))],
+        scratch_shapes=[pltpu.VMEM((n, height, 3 * cols // n), jnp.float32)] * 3 + [
+            pltpu.VMEM((n, height // 2, 3 * cols // n), jnp.bfloat16)] * 2 + [
+            sem((n, steps)), sem((n, steps)), sem((n, steps)), sem((n, steps)),
+            sem((n, steps + 1)), sem((n, steps + 1)), sem((n_lang - 1,)), sem((n_lang - 1,))],
         compiler_params=pltpu.CompilerParams(
             collective_id=0, has_side_effects=True, vmem_limit_bytes=50 * 1024 * 1024),
     )(*kept, *got, dxt)
@@ -369,20 +382,21 @@
     def outer(rows, d):
         return lax.dot_general(rows, d, contract, preferred_element_type=jnp.float32)
 
-    jobs = [
-        (recv_flat, dv_b, high + low + upper),
-        (recv_flat, dk_b, upper + high + low),
-        (own_flat, dq_b, low + upper + high),
+    jobs = [(recv_flat, dv_b), (recv_flat, dk_b), (own_flat, dq_b)]
+    orders = [
+        high + low + upper, high + upper + low,
+        upper + high + low, upper + low + high,
+        low + upper + high, low + high + upper,
     ]
-    got = [swap(outer(rows, half(d, 1 - my[core], 1)), core) for rows, d, _ in jobs]
-    kept = [outer(rows, half(d, my[core], 1)) for rows, d, _ in jobs]
+    got = [swap(outer(rows, half(d, 1 - my[core], 1)), core) for rows, d in jobs]
+    kept = [outer(rows, half(d, my[core], 1)) for rows, d in jobs]
     dxt = jnp.dot(dk_b, w_key.T, preferred_element_type=jnp.float32) + jnp.dot(
         dv_b, w_value.T, preferred_element_type=jnp.float32
     )
     dxt = dxt.reshape(n_lang, cap, length, width)
     factor = 1.0 / (sent_dev * n_lang * n_pair * length) ** 0.5
     grad_wv, grad_wk, grad_wq, ret = reduce_all(
-        n_lang, n_pair, [order for _, _, order in jobs], factor, kept, got, dxt)
+        n_lang, n_pair, orders, factor, kept, got, dxt)
     returned = [dxt[0]] + [ret[d] for d in range(n_lang - 1)]
 
     grad_total = jnp.dot(dq_b, w_query.T, preferred_element_type=jnp.float32).reshape(

time: 221 us -> 203 us (0.919); the launches traced: 219 us -> 207 us
  Pallas kernels: 158 us -> 146 us
    pallas_call x1, Pallas kernels: 128 us -> 111 us  [reduce_all(): pl.pallas_call(functools.partial(reduce_kernel, n_lang, n_pair, orders, f...]
    pallas_call x1, Pallas kernels: 29.8 us -> 34.2 us  [attend(): pl.pallas_call(attend_kernel, grid=(width // GROUP,), in_specs=[smem, sme...]
where the time goes in v4:
time: 203 us; the launch traced here: 207 us
  Pallas kernels  146 us (72%)
  matrix products  25.5 us (13%)
  local copies, waits for them, and re-layouts  9.18 us (5%)
  between operations  8.58 us (4%)
  waiting for transfers between devices  8.29 us (4%)
  other arithmetic  5.91 us (3%)
  starting transfers between devices  3.59 us (2%)
    pallas_call x1, Pallas kernels, reduce_all(): pl.pallas_call(functools.partial(reduce_kernel, n_lang, n_pair, orders, f...  111 us
    pallas_call x1, Pallas kernels, attend(): pl.pallas_call(attend_kernel, grid=(width // GROUP,), in_specs=[smem, sme...  34.2 us
    dot_general x6, matrix products, outer(): lax.dot_general(rows, d, contract, preferred_element_type=jnp.float32)  12.6 us
    ppermute x3, waiting for transfers between devices, exchange(): return lax.ppermute(x, 'lang', [(i, i ^ d) for i in range(n_lang)])  8.28 us
    unnamed x45, local copies, waits for them, and re-layouts  7.44 us
    dot_general x3, matrix products, project(): jnp.dot(rows.reshape(-1, rows.shape[-1]), weight, preferred_element_type=...  6.36 us
  transfers between devices with their start and end apart: 6, of which 2 were waited for; matrix products, arithmetic and copies ran while one was open for 10% of the time, Pallas kernels for 0%

profile of v4, /device:TPU:0, one launch (start us, length us, event | category | flops | bytes accessed | tf_op | source)
XLA Modules:
  0.0 206.6 jit_solution(7173237613814299047)
XLA Ops:
  0.7 1.5 constant_dynamic-slice_fusion.3
  9.9 2.1 %dynamic-slice_select_fusion.3 = (bf16[1,128,1024]{2,1,0:T(8,128)(2,1)S(1)}, bf16[1,128,1024]{2,1,0:T(8,128)(2,1)}, bf16[1,128,1024]{2,1,0:T(8,128)(2,1)}, bf16[1,128,1024]{2,1,0:T(8,128)(2,1)}) fusion(bf16[4,128,1024]{2,1,0:T(8,128)(2,1)} %param.11, s32[]{:T(128)} %bitcast.7, pred[]{:T(512)} %bitcast.6, s32[]{:T(128)} %bitcast.10, pred[]{:T(512)} %bitcast.9, ...), kind=kLoop, calls=%fused_computation.26 | loop fusion | flops 524288 | bytes 2097172 | tf_op jit(solution)/shard_map/jit(_take)/select_n | solution.py:363
  12.0 2.4 %collective-permute-start.2 = (bf16[1,128,1024]{2,1,0:T(8,128)(2,1)}, bf16[1,128,1024]{2,1,0:T(8,128)(2,1)}, u32[]{:S(2)}, u32[]{:S(2)}) collective-permute-start(bf16[1,128,1024]{2,1,0:T(8,128)(2,1)} %get-tuple-element.38), channel_id=1, source_target_pairs={{0,24},{8,16},{16,8},{24,0},{1,25},{9,17},{17,9},{25,1},{2,26},{10... | collective-permute-start | bytes 786440 | tf_op jit(solution)/shard_map/ppermute | solution.py:358
  15.1 3.8 %convolution_convert_fusion.2 = bf16[512,1024]{1,0:T(8,128)(2,1)} fusion(bf16[512,1024]{1,0:T(8,128)(2,1)S(1)} %bitcast.80, bf16[1024,1024]{1,0:T(8,128)(2,1)} %param.13), kind=kOutput, calls=%fused_computation.8 | convolution fusion | flops 1074266112 | bytes 4194304 | tf_op jit(solution)/shard_map/dot_general | solution.py:164
  18.9 2.5 %collective-permute-done.2 = bf16[1,128,1024]{2,1,0:T(8,128)(2,1)} collective-permute-done((bf16[1,128,1024]{2,1,0:T(8,128)(2,1)}, bf16[1,128,1024]{2,1,0:T(8,128)(2,1)}, u32[]{:S(2)}, u32[]{:S(2)}) %collective-permute-start.2) | collective-permute-done | bytes 262176 | tf_op jit(solution)/shard_map/ppermute | solution.py:358
  21.4 5.8 %collective-permute-done.1 = bf16[1,128,1024]{2,1,0:T(8,128)(2,1)} collective-permute-done((bf16[1,128,1024]{2,1,0:T(8,128)(2,1)}, bf16[1,128,1024]{2,1,0:T(8,128)(2,1)}, u32[]{:S(2)}, u32[]{:S(2)}) %collective-permute-start.1) | collective-permute-done | bytes 262176 | tf_op jit(solution)/shard_map/ppermute | solution.py:358
  28.5 1.3 convolution_convert_fusion.1
  30.4 1.3 convolution_convert_fusion
  32.0 34.2 %shard_map.128 = (bf16[4,128,1024]{2,1,0:T(8,128)(2,1)}, bf16[4,128,1024]{2,1,0:T(8,128)(2,1)S(1)}, bf16[4,128,1024]{2,1,0:T(8,128)(2,1)S(1)}, bf16[4,128,1024]{2,1,0:T(8,128)(2,1)S(1)}) custom-call(s32[16]{0:T(128)S(1)} %bitcast.69, s32[16]{0:T(128)S(1)} %xor_bitcast_fusion.slot_ref, s32[16]{0:T(128)S(1)} %bitcast.70, bf16[4,128,1024]{2,1,0:T(8,128)(2,1)S(1)} %bitcast.71, ...), custom_call_target="tpu_custom_call" | custom-call | flops 12000000000 | bytes 30000000 | tf_op jit(solution)/shard_map/pallas_call | solution.py:141
  66.2 2.2 %fusion.5 = f32[1024,512]{1,0:T(8,128)} fusion(bf16[512,1024]{1,0:T(8,128)(2,1)S(1)} %bitcast.76, bf16[512,1024]{1,0:T(8,128)(2,1)S(1)} %bitcast.66, s32[]{:T(128)S(6)} %select_n.66), kind=kOutput, calls=%fused_computation.16 | convolution fusion | flops 536870912 | bytes 3670020 | tf_op jit(solution)/shard_map/dot_general | solution.py:383
  68.4 2.1 %fusion.3 = f32[1024,512]{1,0:T(8,128)} fusion(bf16[512,1024]{1,0:T(8,128)(2,1)S(1)} %bitcast.77, bf16[512,1024]{1,0:T(8,128)(2,1)S(1)} %bitcast.63, s32[]{:T(128)S(6)} %select_n.66), kind=kOutput, calls=%fused_computation.14 | convolution fusion | flops 536870912 | bytes 3670020 | tf_op jit(solution)/shard_map/dot_general | solution.py:383
  71.0 2.1 %convolution_bitcast_fusion = f32[1024,512]{1,0:T(8,128)} fusion(bf16[512,1024]{1,0:T(8,128)(2,1)S(1)} %bitcast.81, bf16[512,1024]{1,0:T(8,128)(2,1)S(1)} %bitcast.61, s32[]{:T(128)S(6)} %select_n.66), kind=kOutput, calls=%fused_computation.3 | convolution fusion | flops 536870912 | bytes 3670020 | tf_op jit(solution)/shard_map/dot_general | solution.py:383
  74.3 1.3 iota_compare_fusion.2
  75.7 2.7 %fusion.18 = f32[512,1024]{1,0:T(8,128)S(1)} fusion(bf16[512,1024]{1,0:T(8,128)(2,1)} %bitcast.64, bf16[1024,1024]{1,0:T(8,128)(2,1)S(1)} %copy-done), kind=kOutput, calls=%fused_computation.42 | convolution fusion | flops 1073741824 | bytes 5242880 | tf_op jit(solution)/shard_map/dot_general | solution.py:393
  78.4 1.3 convolution_add_fusion
  79.8 2.1 %fusion.10.kept0 = f32[1024,512]{1,0:T(8,128)} fusion(bf16[512,1024]{1,0:T(8,128)(2,1)S(1)} %bitcast.78, bf16[512,1024]{1,0:T(8,128)(2,1)S(1)} %bitcast.68, s32[]{:T(128)S(6)} %select_n.65), kind=kOutput, calls=%fused_computation.21 | convolution fusion | flops 536870912 | bytes 3670020 | tf_op jit(solution)/shard_map/dot_general | solution.py:383
  81.8 2.1 %fusion.8.kept1 = f32[1024,512]{1,0:T(8,128)} fusion(bf16[512,1024]{1,0:T(8,128)(2,1)S(1)} %bitcast.79, bf16[512,1024]{1,0:T(8,128)(2,1)S(1)} %bitcast.65, s32[]{:T(128)S(6)} %select_n.65), kind=kOutput, calls=%fused_computation.19 | convolution fusion | flops 536870912 | bytes 3670020 | tf_op jit(solution)/shard_map/dot_general | solution.py:383
  83.9 2.1 %convolution_bitcast_fusion.1.kept2 = f32[1024,512]{1,0:T(8,128)} fusion(bf16[512,1024]{1,0:T(8,128)(2,1)S(1)} %bitcast.82, bf16[512,1024]{1,0:T(8,128)(2,1)S(1)} %bitcast.62, s32[]{:T(128)S(6)} %select_n.65), kind=kOutput, calls=%fused_computation.4 | convolution fusion | flops 536870912 | bytes 3670020 | tf_op jit(solution)/shard_map/dot_general | solution.py:383
  86.0 111.4 %shard_map.129 = (bf16[1024,1024]{1,0:T(8,128)(2,1)S(1)}, bf16[1024,1024]{1,0:T(8,128)(2,1)}, bf16[1024,1024]{1,0:T(8,128)(2,1)}, f32[3,1,128,1024]{3,2,1,0:T(8,128)S(1)}) custom-call(f32[1024,512]{1,0:T(8,128)} %fusion.10.kept0, f32[1024,512]{1,0:T(8,128)} %fusion.8.kept1, f32[1024,512]{1,0:T(8,128)} %convolution_bitcast_fusion.1.kept2, ...), custom_call_target="tpu_custom_call" | custom-call | tf_op jit(solution)/shard_map/pallas_call | solution.py:327
  197.6 1.4 copy-done.19
  199.0 2.7 %add_convert_fusion = bf16[4,128,1024]{2,1,0:T(8,128)(2,1)} fusion(f32[128,1024]{1,0:T(8,128)S(1)} %get-tuple-element.34, f32[128,1024]{1,0:T(8,128)S(1)} %get-tuple-element.35, f32[128,1024]{1,0:T(8,128)S(1)} %get-tuple-element.33, f32[128,1024]{1,0:T(8,128)S(1)} %slice.26, pred[4]{0:T(512)(128)(4,1)S(1)} %get-tuple-element.44, ...), kind=kOutput, calls=%fused_computation.2 | convolution fusion | flops 1078460416 | bytes 6291472 | tf_op jit(solution)/shard_map/dot_general | solution.py:402
  201.6 1.3 copy.21
  204.0 1.3 copy.22
  205.3 1.3 copy.23
  (55 shorter events, 6.0 us)
Async XLA Ops:
  0.6 27.8 %copy-start = (bf16[1024,1024]{1,0:T(8,128)(2,1)S(1)}, bf16[1024,1024]{1,0:T(8,128)(2,1)}, u32[]{:S(2)}) copy-start(bf16[1024,1024]{1,0:T(8,128)(2,1)} %param.14) | copy-start | bytes 6291460
  0.6 14.4 %copy-start.11 = (bf16[4,128,1024]{2,1,0:T(8,128)(2,1)S(1)}, bf16[4,128,1024]{2,1,0:T(8,128)(2,1)}, u32[]{:S(2)}) copy-start(bf16[4,128,1024]{2,1,0:T(8,128)(2,1)} %param.11) | copy-start | bytes 3145732
  12.0 9.4 %collective-permute-start.2 = (bf16[1,128,1024]{2,1,0:T(8,128)(2,1)}, bf16[1,128,1024]{2,1,0:T(8,128)(2,1)}, u32[]{:S(2)}, u32[]{:S(2)}) collective-permute-start(bf16[1,128,1024]{2,1,0:T(8,128)(2,1)} %get-tuple-element.38), channel_id=1, source_target_pairs={{0,24},{8,16},{16,8},{24,0},{1,25},{9,17},{17,9},{25,1},{2,26},{10... | collective-permute-start | bytes 786440 | tf_op jit(solution)/shard_map/ppermute | solution.py:358
  14.4 12.8 %collective-permute-start.1 = (bf16[1,128,1024]{2,1,0:T(8,128)(2,1)}, bf16[1,128,1024]{2,1,0:T(8,128)(2,1)}, u32[]{:S(2)}, u32[]{:S(2)}) collective-permute-start(bf16[1,128,1024]{2,1,0:T(8,128)(2,1)} %get-tuple-element.39), channel_id=1, source_target_pairs={{0,16},{8,24},{16,0},{24,8},{1,17},{9,25},{17,1},{25,9},{2,18},{10... | collective-permute-start | bytes 786440 | tf_op jit(solution)/shard_map/ppermute | solution.py:358
  15.0 12.2 %collective-permute-start = (bf16[1,128,1024]{2,1,0:T(8,128)(2,1)}, bf16[1,128,1024]{2,1,0:T(8,128)(2,1)}, u32[]{:S(2)}, u32[]{:S(2)}) collective-permute-start(bf16[1,128,1024]{2,1,0:T(8,128)(2,1)} %get-tuple-element.37), channel_id=1, source_target_pairs={{0,8},{8,0},{16,24},{24,16},{1,9},{9,1},{17,25},{25,17},{2,10},{10... | collective-permute-start | bytes 786440 | tf_op jit(solution)/shard_map/ppermute | solution.py:358
  15.1 3.8 %copy-start.20 = (s32[1,16]{1,0:T(1,128)S(1)}, s32[1,16]{1,0:T(1,128)}, u32[]{:S(2)}) copy-start(s32[1,16]{1,0:T(1,128)} %param.18) | copy-start | bytes 196
  28.4 39.9 %copy-start.9 = (bf16[4,128,1024]{2,1,0:T(8,128)(2,1)}, bf16[4,128,1024]{2,1,0:T(8,128)(2,1)S(1)}, u32[]{:S(2)}) copy-start(bf16[4,128,1024]{2,1,0:T(8,128)(2,1)S(1)} %pad_maximum_fusion) | copy-start | bytes 3145732
  28.5 2.0 copy-start.17
  30.4 1.6 copy-start.8
  66.2 2.2 %copy-start.3 = (bf16[4,128,1024]{2,1,0:T(8,128)(2,1)}, bf16[4,128,1024]{2,1,0:T(8,128)(2,1)S(1)}, u32[]{:S(2)}) copy-start(bf16[4,128,1024]{2,1,0:T(8,128)(2,1)S(1)} %get-tuple-element.17) | copy-start | bytes 3145732
  66.2 2.2 %copy-start.1 = (bf16[4,128,1024]{2,1,0:T(8,128)(2,1)}, bf16[4,128,1024]{2,1,0:T(8,128)(2,1)S(1)}, u32[]{:S(2)}) copy-start(bf16[4,128,1024]{2,1,0:T(8,128)(2,1)S(1)} %get-tuple-element.16) | copy-start | bytes 3145732
  68.3 17.7 %collective-permute-start.3 = (f32[1024,512]{1,0:T(8,128)}, f32[1024,512]{1,0:T(8,128)}, u32[]{:S(2)}, u32[]{:S(2)}) collective-permute-start(f32[1024,512]{1,0:T(8,128)} %fusion.5), channel_id=1, source_target_pairs={{0,8},{1,9},{2,10},{3,11},{4,12},{5,13},{6,14},{7,15},{8,0},{9,1},... | collective-permute-start | bytes 6291464 | tf_op jit(solution)/shard_map/ppermute | solution.py:175
  68.4 2.6 %copy-start.12 = (bf16[4,128,1024]{2,1,0:T(8,128)(2,1)S(1)}, bf16[4,128,1024]{2,1,0:T(8,128)(2,1)}, u32[]{:S(2)}) copy-start(bf16[4,128,1024]{2,1,0:T(8,128)(2,1)} %param.11) | copy-start | bytes 3145732
  70.5 15.5 %collective-permute-start.4 = (f32[1024,512]{1,0:T(8,128)}, f32[1024,512]{1,0:T(8,128)}, u32[]{:S(2)}, u32[]{:S(2)}) collective-permute-start(f32[1024,512]{1,0:T(8,128)} %fusion.3), channel_id=1, source_target_pairs={{0,8},{1,9},{2,10},{3,11},{4,12},{5,13},{6,14},{7,15},{8,0},{9,1},... | collective-permute-start | bytes 6291464 | tf_op jit(solution)/shard_map/ppermute | solution.py:175
  73.1 12.9 %collective-permute-start.5 = (f32[1024,512]{1,0:T(8,128)}, f32[1024,512]{1,0:T(8,128)}, u32[]{:S(2)}, u32[]{:S(2)}) collective-permute-start(f32[1024,512]{1,0:T(8,128)} %convolution_bitcast_fusion), channel_id=1, source_target_pairs={{0,8},{1,9},{2,10},{3,11},{4,12},{5,13},{6,14},{7,15},{8,0},{9,1},... | collective-permute-start | bytes 6291464 | tf_op jit(solution)/shard_map/ppermute | solution.py:175
  75.7 2.7 %copy-start.4 = (bf16[4,128,1024]{2,1,0:T(8,128)(2,1)S(1)}, bf16[4,128,1024]{2,1,0:T(8,128)(2,1)}, u32[]{:S(2)}) copy-start(bf16[4,128,1024]{2,1,0:T(8,128)(2,1)} %copy-done.3) | copy-start | bytes 3145732
  75.7 2.7 %copy-start.18 = (bf16[1024,1024]{1,0:T(8,128)(2,1)S(1)}, bf16[1024,1024]{1,0:T(8,128)(2,1)}, u32[]{:S(2)}) copy-start(bf16[1024,1024]{1,0:T(8,128)(2,1)} %param.15) | copy-start | bytes 6291460
  78.4 1.4 copy-start.10
  79.7 2.2 %copy-start.14 = (f32[512,1024]{1,0:T(8,128)}, f32[512,1024]{1,0:T(8,128)S(1)}, u32[]{:S(2)}) copy-start(f32[512,1024]{1,0:T(8,128)S(1)} %convolution_add_fusion) | copy-start | bytes 6291460
  79.8 2.1 %copy-start.2 = (bf16[4,128,1024]{2,1,0:T(8,128)(2,1)S(1)}, bf16[4,128,1024]{2,1,0:T(8,128)(2,1)}, u32[]{:S(2)}) copy-start(bf16[4,128,1024]{2,1,0:T(8,128)(2,1)} %copy-done.1) | copy-start | bytes 3145732
  81.8 2.1 %copy-start.13 = (bf16[4,128,1024]{2,1,0:T(8,128)(2,1)S(1)}, bf16[4,128,1024]{2,1,0:T(8,128)(2,1)}, u32[]{:S(2)}) copy-start(bf16[4,128,1024]{2,1,0:T(8,128)(2,1)} %param.11) | copy-start | bytes 3145732
  197.4 1.6 copy-start.19
  199.0 2.7 %copy-start.16 = (bf16[1024,1024]{1,0:T(8,128)(2,1)S(1)}, bf16[1024,1024]{1,0:T(8,128)(2,1)}, u32[]{:S(2)}) copy-start(bf16[1024,1024]{1,0:T(8,128)(2,1)} %get-tuple-element.55) | copy-start | bytes 6291460
  201.6 2.3 %copy-start.15 = (bf16[1024,1024]{1,0:T(8,128)(2,1)S(1)}, bf16[1024,1024]{1,0:T(8,128)(2,1)}, u32[]{:S(2)}) copy-start(bf16[1024,1024]{1,0:T(8,128)(2,1)} %get-tuple-element.56) | copy-start | bytes 6291460
  (3 other events, 3.9 us)
